TPU v7x, 32 devices: a whole 2x2x4 slice. The times are simulated.
32 devices in a mesh: seq: 4 (over x, core), rows: 8 (over z, y).
Axes of the slice: x: 2, y: 2, z: 4, core: 2. Of those that a mesh axis runs over, the one named last changes fastest.
Arguments:
- blocks: bfloat16 [32, 1024, 768], P('rows', 'seq'), may hold values from -6 to 6
- segment_ids: int32 [32, 1024], P('rows', 'seq'), may hold values from 0 to 129, as said below
- cotangent: bfloat16 [32, 1024, 768], P('rows', 'seq'), may hold values from -6 to 6
- w_query: bfloat16 [768, 768], replicated, may hold values from -0.3125 to 0.3125
- w_key: bfloat16 [768, 768], replicated, may hold values from -0.3125 to 0.3125
- w_value: bfloat16 [768, 768], replicated, may hold values from -0.21875 to 0.21875
- w_out: bfloat16 [768, 768], replicated, may hold values from -0.625 to 0.625
- norm_one: float32 [768], replicated, may hold values from 0.1 to 1.9
- norm_two: float32 [768], replicated, may hold values from 0.1 to 1.9
- w_gate: bfloat16 [768, 2048], replicated, may hold values from -0.21875 to 0.21875
- w_up: bfloat16 [768, 2048], replicated, may hold values from -0.21875 to 0.21875
- w_down: bfloat16 [2048, 768], replicated, may hold values from -0.125 to 0.125
Outputs:
- output: bfloat16 [32, 1024, 768], P('rows', 'seq')
- d_blocks: bfloat16 [32, 1024, 768], P('rows', 'seq')
- d_w_query: float32 [768, 768], replicated
- d_w_key: float32 [768, 768], replicated
- d_w_value: float32 [768, 768], replicated
- d_w_out: float32 [768, 768], replicated
- d_norm_one: float32 [768], replicated
- d_norm_two: float32 [768], replicated
- d_w_gate: float32 [768, 2048], replicated
- d_w_up: float32 [768, 2048], replicated
- d_w_down: float32 [2048, 768], replicated
Inputs may be any that keep to these rules, and one draw needn't show every extreme that they name: `segment_ids`: ids never fall along a row and each row begins with 0; equal ids in a row mark one document, and the segments after a row's longest document are short documents and padding. In every row one document has its first block at an index from 1 to 128 and its last block at an index from 895 to 1024 - 2 (block indices counted from 0).
All inputs are finite; a program needn't handle non-finite values.
Results may differ from a plain program's by a relative error of at most 0.019.
Values may be sent and summed in bfloat16 or wider, within the bound.
A program may use at most 384 MiB of HBM per device.

v0:
```python
from functools import partial

import jax
import jax.numpy as jnp
from jax import lax
from jax.sharding import PartitionSpec as P

HEAD_DIM = 64


EPSILON = 1e-06
MASKED = -1000000000.0


def rms_norm(value, gain):
    return value * lax.rsqrt(jnp.mean(value * value, axis=-1, keepdims=True) + EPSILON) * gain


def outer_sum(left, right):
    return lax.dot_general(
        left, right, (((0,), (0,)), ((), ())), preferred_element_type=jnp.float32
    )


def back_project(gradient, weight):
    return lax.dot_general(
        gradient, weight, (((1,), (1,)), ((), ())), preferred_element_type=jnp.float32
    )


def probabilities(query_part, keys_all, same_doc):
    scores = jnp.einsum(
        "rqhd,rkhd->rhqk", query_part, keys_all, preferred_element_type=jnp.float32
    ) * HEAD_DIM ** (-0.5)
    scores = jnp.where(same_doc, scores, MASKED)
    largest = jnp.max(scores, axis=-1, keepdims=True)
    exponent = jnp.exp(scores - largest)
    total = jnp.sum(exponent, axis=-1, keepdims=True)
    return (exponent / total, largest, total)


def body(
    blocks,
    segment_ids,
    cotangent,
    w_query,
    w_key,
    w_value,
    w_out,
    norm_one,
    norm_two,
    w_gate,
    w_up,
    w_down,
):
    row_count, positions, features = blocks.shape
    token_count = row_count * positions
    head_count = features // HEAD_DIM
    x_flat = blocks.astype(jnp.float32).reshape(token_count, features)
    normed_one = rms_norm(x_flat, norm_one).astype(jnp.bfloat16)

    def project(weight):
        made = jnp.dot(normed_one, weight, preferred_element_type=jnp.float32)
        return made.astype(jnp.bfloat16).reshape(row_count, positions, head_count, HEAD_DIM)

    query_part = project(w_query)
    key_part = project(w_key)
    value_part = project(w_value)
    keys_all, values_all, ids_all = (
        lax.all_gather(key_part, "seq", axis=1, tiled=True),
        lax.all_gather(value_part, "seq", axis=1, tiled=True),
        lax.all_gather(segment_ids, "seq", axis=1, tiled=True),
    )
    same_doc = segment_ids[:, None, :, None] == ids_all[:, None, None, :]
    forward_probs = probabilities(query_part, keys_all, same_doc)[0].astype(jnp.bfloat16)
    mixed_heads = jnp.einsum(
        "rhqk,rkhd->rqhd", forward_probs, values_all, preferred_element_type=jnp.float32
    )
    mixed_heads = mixed_heads.astype(jnp.bfloat16).reshape(token_count, features)
    x_one = x_flat + jnp.dot(mixed_heads, w_out, preferred_element_type=jnp.float32)
    normed_two = rms_norm(x_one, norm_two).astype(jnp.bfloat16)
    gate_value = jnp.dot(normed_two, w_gate, preferred_element_type=jnp.float32)
    up_value = jnp.dot(normed_two, w_up, preferred_element_type=jnp.float32)
    activated, gelu_back = jax.vjp(partial(jax.nn.gelu, approximate=True), gate_value)
    hidden = (activated * up_value).astype(jnp.bfloat16)
    output_sum = x_one + jnp.dot(hidden, w_down, preferred_element_type=jnp.float32)
    result = output_sum.astype(jnp.bfloat16).reshape(row_count, positions, features)
    grad_low = cotangent.reshape(token_count, features)
    gradient = grad_low.astype(jnp.float32)
    d_down = outer_sum(hidden, grad_low)
    d_hidden = back_project(grad_low, w_down)
    d_gate = gelu_back(d_hidden * up_value)[0].astype(jnp.bfloat16)
    d_up = (d_hidden * activated).astype(jnp.bfloat16)
    d_gate_w = outer_sum(normed_two, d_gate)
    d_up_w = outer_sum(normed_two, d_up)
    d_normed_two = back_project(d_gate, w_gate) + back_project(d_up, w_up)
    norm_two_pull = jax.vjp(rms_norm, x_one, norm_two)[1]
    d_x_part, d_norm_two = norm_two_pull(d_normed_two)
    d_x_one = gradient + d_x_part
    d_branch = d_x_one.astype(jnp.bfloat16)
    d_out_w = outer_sum(mixed_heads, d_branch)
    d_mixed = (
        back_project(d_branch, w_out)
        .astype(jnp.bfloat16)
        .reshape(row_count, positions, head_count, HEAD_DIM)
    )
    probability, largest, total = probabilities(query_part, keys_all, same_doc)
    d_probs = jnp.einsum("rqhd,rkhd->rhqk", d_mixed, values_all, preferred_element_type=jnp.float32)
    weighted = jnp.sum(probability * d_probs, axis=-1, keepdims=True)
    d_scores = (probability * (d_probs - weighted)).astype(jnp.bfloat16)
    scale = HEAD_DIM ** (-0.5)
    d_query = (
        jnp.einsum("rhqk,rkhd->rqhd", d_scores, keys_all, preferred_element_type=jnp.float32)
        * scale
    )
    d_query = d_query.astype(jnp.bfloat16).reshape(token_count, features)
    d_key_term = (
        jnp.einsum("rhqk,rqhd->rkhd", d_scores, query_part, preferred_element_type=jnp.float32)
        * scale
    )
    d_value_term = jnp.einsum(
        "rhqk,rqhd->rkhd",
        probability.astype(jnp.bfloat16),
        d_mixed,
        preferred_element_type=jnp.float32,
    )
    d_key_sum, d_value_sum = (
        lax.psum_scatter(
            d_key_term.astype(jnp.bfloat16), "seq", scatter_dimension=1, tiled=True
        ).astype(jnp.float32),
        lax.psum_scatter(
            d_value_term.astype(jnp.bfloat16), "seq", scatter_dimension=1, tiled=True
        ).astype(jnp.float32),
    )
    d_key = d_key_sum.astype(jnp.bfloat16).reshape(token_count, features)
    d_value = d_value_sum.astype(jnp.bfloat16).reshape(token_count, features)
    d_query_w = outer_sum(normed_one, d_query)
    d_key_w = outer_sum(normed_one, d_key)
    d_value_w = outer_sum(normed_one, d_value)
    d_normed_one = (
        back_project(d_query, w_query) + back_project(d_key, w_key) + back_project(d_value, w_value)
    )
    norm_one_pull = jax.vjp(rms_norm, x_flat, norm_one)[1]
    d_x_first, d_norm_one = norm_one_pull(d_normed_one)
    d_input = (d_x_one + d_x_first).astype(jnp.bfloat16).reshape(row_count, positions, features)
    grad_shares = (
        lax.psum_scatter(d_query_w, "rows", scatter_dimension=0, tiled=True),
        lax.psum_scatter(d_key_w, "rows", scatter_dimension=0, tiled=True),
        lax.psum_scatter(d_value_w, "rows", scatter_dimension=0, tiled=True),
        lax.psum_scatter(d_out_w, "rows", scatter_dimension=0, tiled=True),
        lax.psum_scatter(d_norm_one, "rows", scatter_dimension=0, tiled=True),
        lax.psum_scatter(d_norm_two, "rows", scatter_dimension=0, tiled=True),
        lax.psum_scatter(d_gate_w, "rows", scatter_dimension=0, tiled=True),
        lax.psum_scatter(d_up_w, "rows", scatter_dimension=0, tiled=True),
        lax.psum_scatter(d_down, "rows", scatter_dimension=0, tiled=True),
    )
    grad_summed = (
        lax.psum(grad_shares[0].astype(jnp.bfloat16), "seq").astype(jnp.float32),
        lax.psum(grad_shares[1].astype(jnp.bfloat16), "seq").astype(jnp.float32),
        lax.psum(grad_shares[2].astype(jnp.bfloat16), "seq").astype(jnp.float32),
        lax.psum(grad_shares[3].astype(jnp.bfloat16), "seq").astype(jnp.float32),
        lax.psum(grad_shares[4].astype(jnp.bfloat16), "seq").astype(jnp.float32),
        lax.psum(grad_shares[5].astype(jnp.bfloat16), "seq").astype(jnp.float32),
        lax.psum(grad_shares[6].astype(jnp.bfloat16), "seq").astype(jnp.float32),
        lax.psum(grad_shares[7].astype(jnp.bfloat16), "seq").astype(jnp.float32),
        lax.psum(grad_shares[8].astype(jnp.bfloat16), "seq").astype(jnp.float32),
    )
    grad_whole = (
        lax.all_gather(grad_summed[0].astype(jnp.bfloat16), "rows", axis=0, tiled=True).astype(
            jnp.float32
        ),
        lax.all_gather(grad_summed[1].astype(jnp.bfloat16), "rows", axis=0, tiled=True).astype(
            jnp.float32
        ),
        lax.all_gather(grad_summed[2].astype(jnp.bfloat16), "rows", axis=0, tiled=True).astype(
            jnp.float32
        ),
        lax.all_gather(grad_summed[3].astype(jnp.bfloat16), "rows", axis=0, tiled=True).astype(
            jnp.float32
        ),
        lax.all_gather(grad_summed[4].astype(jnp.bfloat16), "rows", axis=0, tiled=True).astype(
            jnp.float32
        ),
        lax.all_gather(grad_summed[5].astype(jnp.bfloat16), "rows", axis=0, tiled=True).astype(
            jnp.float32
        ),
        lax.all_gather(grad_summed[6].astype(jnp.bfloat16), "rows", axis=0, tiled=True).astype(
            jnp.float32
        ),
        lax.all_gather(grad_summed[7].astype(jnp.bfloat16), "rows", axis=0, tiled=True).astype(
            jnp.float32
        ),
        lax.all_gather(grad_summed[8].astype(jnp.bfloat16), "rows", axis=0, tiled=True).astype(
            jnp.float32
        ),
    )
    return (
        result,
        d_input,
        grad_whole[0],
        grad_whole[1],
        grad_whole[2],
        grad_whole[3],
        grad_whole[4],
        grad_whole[5],
        grad_whole[6],
        grad_whole[7],
        grad_whole[8],
    )


def solution(mesh):
    placed = (
        P("rows", "seq", None),
        P("rows", "seq"),
        P("rows", "seq", None),
        P(),
        P(),
        P(),
        P(),
        P(),
        P(),
        P(),
        P(),
        P(),
    )
    return jax.shard_map(
        body,
        mesh=mesh,
        in_specs=placed,
        out_specs=(
            P("rows", "seq", None),
            P("rows", "seq", None),
            P(),
            P(),
            P(),
            P(),
            P(),
            P(),
            P(),
            P(),
            P(),
        ),
        check_vma=False,
    )
```

profile of v0, /device:TPU:0, one launch (start us, length us, event | category | flops | bytes accessed | tf_op | source)
XLA Modules:
  0.0 1446.7 jit_solution(8277974285765861284)
XLA Ops:
  19.1 3.9 reshape.150
  25.8 4.3 convolution_convert_fusion.3
  32.7 3.9 reshape.148
  39.7 4.3 convolution_convert_fusion.2
  46.7 3.9 reshape.149
  50.5 6.3 all_gather.37
  58.5 17.5 %all-gather.12.cloned.1.call-done = bf16[4,1024,12,64]{1,3,2,0:T(8,128)(2,1)} async-done(((bf16[4,256,12,64]{1,3,2,0:T(8,128)(2,1)}), bf16[4,1024,12,64]{1,3,2,0:T(8,128)(2,1)}) %all-gather.12.cloned.1.call-update) | async-done | bytes 6291472 | tf_op jit(solution)/shard_map/all_gather | solution.py:70
  75.9 27.5 %fusion.59 = (f32[4,12,256]{2,1,0:T(8,128)S(1)}, f32[4,12,256,1024]{3,2,1,0:T(8,128)}) fusion(pred[4,256,1024]{2,1,0:T(8,128)(4,1)} %broadcast_compare_fusion, bf16[4,1024,12,64]{1,3,2,0:T(8,128)(2,1)} %all-gather.12.cloned.1.call-done, bf16[4,256,12,64]{1,0,3,2:T(4,128)(2,1)} %reshape.149), kind=kOutput, calls=%fused_computation.87 | convolution fusion | flops 1660945408 | bytes 59293696 | tf_op jit(solution)/shard_map/sub | solution.py:37
  103.5 21.9 %all-gather.10.cloned.1.call-done = bf16[4,1024,12,64]{1,3,2,0:T(8,128)(2,1)} async-done(((bf16[4,256,12,64]{1,3,2,0:T(8,128)(2,1)}), bf16[4,1024,12,64]{1,3,2,0:T(8,128)(2,1)}) %all-gather.10.cloned.1.call-update) | async-done | bytes 6291472 | tf_op jit(solution)/shard_map/all_gather | solution.py:71
  125.3 21.3 %fusion.35 = bf16[4,256,12,64]{1,3,2,0:T(8,128)(2,1)} fusion(bf16[4,1024,12,64]{1,3,2,0:T(8,128)(2,1)} %all-gather.10.cloned.1.call-done, f32[4,12,256,1024]{3,2,1,0:T(8,128)} %get-tuple-element.36, f32[4,12,256]{2,1,0:T(8,128)S(1)} %get-tuple-element.35), kind=kOutput, calls=%fused_computation.63 | convolution fusion | flops 1636564992 | bytes 58245120 | tf_op jit(solution)/shard_map/rhqk,rkhd->rqhd/dot_general | solution.py:76
  154.6 5.6 fusion.65
  160.2 6.0 fusion.64
  166.2 13.8 multiply_convert_fusion.2
  180.0 6.9 fusion.66
  186.9 4.5 multiply_reduce_fusion.1
  199.2 4.2 reshape.154
  203.4 20.6 %convert_bitcast_fusion = bf16[4,1024,12,64]{1,3,2,0:T(8,128)(2,1)} fusion(bf16[4,256,12,64]{1,0,3,2:T(4,128)(2,1)} %reshape.154, f32[4,12,256,1024]{3,2,1,0:T(8,128)} %get-tuple-element.36, f32[4,12,256]{2,1,0:T(8,128)S(1)} %get-tuple-element.35), kind=kOutput, calls=%fused_computation.29 | convolution fusion | flops 1638924288 | bytes 58245120 | tf_op jit(solution)/shard_map/rhqk,rqhd->rkhd/dot_general | solution.py:121
  224.1 38.2 %multiply_reduce_fusion = (f32[4,12,256]{2,1,0:T(8,128)S(1)}, f32[4,12,256,1024]{3,2,1,0:T(8,128)}) fusion(f32[4,12,256,1024]{3,2,1,0:T(8,128)} %get-tuple-element.36, f32[4,12,256]{2,1,0:T(8,128)S(1)} %get-tuple-element.35, bf16[4,1024,12,64]{1,3,2,0:T(8,128)(2,1)} %all-gather.10.cloned.1.call-done, bf16[4,256,12,64]{1,0,3,2:T(4,128)(2,1)} %reshape.154), kind=kOutput, calls=%fused_computation.2 | convolution fusion | flops 1648349184 | bytes 108625920 | tf_op jit(solution)/shard_map/rqhd,rkhd->rhqk/dot_general | solution.py:108
  262.3 40.4 %multiply_convert_fusion = bf16[4,12,256,1024]{3,2,1,0:T(8,128)(2,1)} fusion(f32[4,12,256,1024]{3,2,1,0:T(8,128)} %get-tuple-element.41, f32[4,12,256]{2,1,0:T(8,128)S(1)} %get-tuple-element.40, f32[4,12,256,1024]{3,2,1,0:T(8,128)} %get-tuple-element.36, f32[4,12,256]{2,1,0:T(8,128)S(1)} %get-tuple-element.35), kind=kLoop, calls=%fused_computation.1 | loop fusion | flops 50331648 | bytes 125927424 | tf_op jit(solution)/shard_map/convert_element_type | solution.py:110
  302.8 15.8 %fusion.18 = bf16[4,1024,12,64]{1,3,2,0:T(8,128)(2,1)} fusion(bf16[4,12,256,1024]{3,2,1,0:T(8,128)(2,1)} %multiply_convert_fusion, bf16[4,256,12,64]{1,0,3,2:T(4,128)(2,1)} %reshape.149), kind=kOutput, calls=%fused_computation.28 | convolution fusion | flops 1616904192 | bytes 33030144 | tf_op jit(solution)/shard_map/rhqk,rqhd->rkhd/dot_general | solution.py:118
  318.7 5.2 fusion.50
  327.2 16.6 %fusion.38 = bf16[4,256,12,64]{1,3,2,0:T(8,128)(2,1)} fusion(bf16[4,1024,12,64]{1,3,2,0:T(8,128)(2,1)} %all-gather.12.cloned.1.call-done, bf16[4,12,256,1024]{3,2,1,0:T(8,128)(2,1)} %multiply_convert_fusion), kind=kOutput, calls=%fused_computation.64 | convolution fusion | flops 1612185600 | bytes 33030144 | tf_op jit(solution)/shard_map/rhqk,rkhd->rqhd/dot_general | solution.py:113
  351.0 8.9 fusion.74
  360.2 8.8 fusion.73
  369.1 8.8 fusion.72
  392.7 57.3 %reduce-scatter.20.cloned.1.call-done = f32[96,768]{1,0:T(8,128)} async-done(((f32[768,768]{1,0:T(8,128)}), f32[96,768]{1,0:T(8,128)}) %reduce-scatter.20.cloned.1.call-update) | async-done | bytes 294928 | tf_op jit(solution)/shard_map/reduce_scatter | solution.py:150
  451.6 70.4 %reduce-scatter.14.cloned.1.call-done = f32[96,768]{1,0:T(8,128)} async-done(((f32[768,768]{1,0:T(8,128)}), f32[96,768]{1,0:T(8,128)}) %reduce-scatter.14.cloned.1.call-update) | async-done | bytes 294928 | tf_op jit(solution)/shard_map/reduce_scatter | solution.py:147
  523.7 119.0 %reduce-scatter.26.cloned.1.call-done = f32[256,768]{1,0:T(8,128)} async-done(((f32[2048,768]{1,0:T(8,128)}), f32[256,768]{1,0:T(8,128)}) %reduce-scatter.26.cloned.1.call-update) | async-done | bytes 786448 | tf_op jit(solution)/shard_map/reduce_scatter | solution.py:155
  644.6 118.8 %reduce-scatter.24.cloned.1.call-done = f32[96,2048]{1,0:T(8,128)} async-done(((f32[768,2048]{1,0:T(8,128)}), f32[96,2048]{1,0:T(8,128)}) %reduce-scatter.24.cloned.1.call-update) | async-done | bytes 786448 | tf_op jit(solution)/shard_map/reduce_scatter | solution.py:154
  765.3 119.4 %reduce-scatter.22.cloned.1.call-done = f32[96,2048]{1,0:T(8,128)} async-done(((f32[768,2048]{1,0:T(8,128)}), f32[96,2048]{1,0:T(8,128)}) %reduce-scatter.22.cloned.1.call-update) | async-done | bytes 786448 | tf_op jit(solution)/shard_map/reduce_scatter | solution.py:153
  886.6 70.4 %reduce-scatter.18.cloned.1.call-done = f32[96,768]{1,0:T(8,128)} async-done(((f32[768,768]{1,0:T(8,128)}), f32[96,768]{1,0:T(8,128)}) %reduce-scatter.18.cloned.1.call-update) | async-done | bytes 294928 | tf_op jit(solution)/shard_map/reduce_scatter | solution.py:149
  958.6 70.7 %reduce-scatter.16.cloned.1.call-done = f32[96,768]{1,0:T(8,128)} async-done(((f32[768,768]{1,0:T(8,128)}), f32[96,768]{1,0:T(8,128)}) %reduce-scatter.16.cloned.1.call-update) | async-done | bytes 294928 | tf_op jit(solution)/shard_map/reduce_scatter | solution.py:148
  1031.0 48.4 %all-reduce.10.cloned.1.call-done = (bf16[96,768]{1,0:T(8,128)(2,1)}, bf16[96,768]{1,0:T(8,128)(2,1)}, bf16[96,768]{1,0:T(8,128)(2,1)}, bf16[96,768]{1,0:T(8,128...) async-done(((bf16[96,768]{1,0:T(8,128)(2,1)}, bf16[96,768]{1,0:T(8,128)(2,1)}, bf16[96,768]{1,0:T(8,128)(2,1)}, ...) | async-done | bytes 1769488 | tf_op jit(solution)/shard_map/psum | solution.py:158
  1088.9 4.5 add_convert_fusion
  1095.6 3.8 fusion.27
  1099.4 21.7 %all-reduce.4 = (bf16[768]{0:T(1024)(128)(2,1)S(1)}, bf16[768]{0:T(1024)(128)(2,1)S(1)}) all-reduce(f32[768]{0:T(1024)S(1)} %get-tuple-element.13, f32[768]{0:T(1024)S(1)} %copy-done.29), channel_id=8, replica_groups=mesh['seq'=4,'rows'=8] {'rows'}, use_global_device_ids=true, to_apply=%region_18.19.clone | all-reduce | flops 1536 | bytes 9216
  1121.3 5.6 all-reduce.6
  1127.4 17.6 %all-reduce.5 = (bf16[768]{0:T(1024)(128)(2,1)S(1)}, bf16[768]{0:T(1024)(128)(2,1)S(1)}) all-reduce(bf16[768]{0:T(1024)(128)(2,1)S(1)} %dynamic-update-slice, bf16[768]{0:T(1024)(128)(2,1)S(1)} %dynamic-update-slice.1), channel_id=1, replica_groups=mesh['seq'=4,'rows'=8] {'rows'}, use_global_device_ids=true, to_apply=%add | all-reduce | flops 1536 | bytes 6144
  1146.2 5.3 fusion.23
  1154.3 11.3 all-gather.18.cloned.1.call-done
  1168.4 39.3 %all-gather.16.cloned.1.call-done = bf16[768,768]{1,0:T(8,128)(2,1)} async-done(((bf16[96,768]{1,0:T(8,128)(2,1)}), bf16[768,768]{1,0:T(8,128)(2,1)}) %all-gather.16.cloned.1.call-update) | async-done | bytes 1179664 | tf_op jit(solution)/shard_map/all_gather | solution.py:172
  1210.5 39.3 %all-gather.14.cloned.1.call-done = bf16[768,768]{1,0:T(8,128)(2,1)} async-done(((bf16[96,768]{1,0:T(8,128)(2,1)}), bf16[768,768]{1,0:T(8,128)(2,1)}) %all-gather.14.cloned.1.call-update) | async-done | bytes 1179664 | tf_op jit(solution)/shard_map/all_gather | solution.py:169
  1252.7 58.7 %all-gather.26.cloned.1.call-done = bf16[2048,768]{1,0:T(8,128)(2,1)} async-done(((bf16[256,768]{1,0:T(8,128)(2,1)}), bf16[2048,768]{1,0:T(8,128)(2,1)}) %all-gather.26.cloned.1.call-update) | async-done | bytes 3145744 | tf_op jit(solution)/shard_map/all_gather | solution.py:193
  1311.3 5.1 convert_element_type.199
  1316.4 56.3 %all-gather.24.cloned.1.call-done = bf16[768,2048]{1,0:T(8,128)(2,1)} async-done(((bf16[96,2048]{1,0:T(8,128)(2,1)}), bf16[768,2048]{1,0:T(8,128)(2,1)}) %all-gather.24.cloned.1.call-update) | async-done | bytes 3145744 | tf_op jit(solution)/shard_map/all_gather | solution.py:190
  1372.7 5.4 convert_element_type.197
  1378.2 56.1 %all-gather.22.cloned.1.call-done = bf16[768,2048]{1,0:T(8,128)(2,1)} async-done(((bf16[96,2048]{1,0:T(8,128)(2,1)}), bf16[768,2048]{1,0:T(8,128)(2,1)}) %all-gather.22.cloned.1.call-update) | async-done | bytes 3145744 | tf_op jit(solution)/shard_map/all_gather | solution.py:187
  1434.2 5.4 convert_element_type.195
  (171 shorter events, 101.7 us)
Async XLA Ops:
  7.2 159.0 %copy-start = (bf16[2048,768]{1,0:T(8,128)(2,1)S(1)}, bf16[2048,768]{1,0:T(8,128)(2,1)}, u32[]{:S(2)}) copy-start(bf16[2048,768]{1,0:T(8,128)(2,1)} %param.23) | copy-start | bytes 9437188
  7.2 68.8 %all-gather.12.cloned.1.call-start = ((), (), s32[]{:S(2)}) async-start(), calls=%async_computation.10 | async-start | bytes 7864320 | tf_op jit(solution)/shard_map/all_gather | solution.py:70
  7.2 6.7 copy-start.35
  25.8 99.5 %all-gather.10.cloned.1.call-start = ((), (), s32[]{:S(2)}) async-start(), calls=%async_computation.9 | async-start | bytes 7864320 | tf_op jit(solution)/shard_map/all_gather | solution.py:71
  39.7 338.4 %reduce-scatter.12.cloned.1.call-start = ((), (), s32[]{:S(2)}) async-start(), calls=%async_computation.12 | async-start | bytes 7864320 | tf_op jit(solution)/shard_map/reduce_scatter | solution.py:131
  44.1 6.5 copy-start.27
  146.6 3.2 copy-start.1
  146.6 3.2 copy-start.34
  149.8 1.7 copy-start.26
  151.5 39.9 %copy-start.5 = (f32[1024,768]{1,0:T(8,128)}, f32[1024,768]{1,0:T(8,128)S(1)}, u32[]{:S(2)}) copy-start(f32[1024,768]{1,0:T(8,128)S(1)} %get-tuple-element.38) | copy-start | bytes 9437188
  151.5 3.0 copy-start.32
  154.6 5.7 copy-start.3
  154.6 5.7 copy-start.31
  160.2 6.0 copy-start.19
  180.0 6.9 copy-start.9
  180.0 6.9 copy-start.10
  180.0 6.9 copy-start.33
  224.0 161.5 %reduce-scatter.10.cloned.1.call-start = ((), (), s32[]{:S(2)}) async-start(), calls=%async_computation.11 | async-start | bytes 7864320 | tf_op jit(solution)/shard_map/reduce_scatter | solution.py:128
  318.6 5.3 copy-start.21
  318.6 5.3 copy-start.28
  318.6 131.4 %reduce-scatter.20.cloned.1.call-start = ((), (), s32[]{:S(2)}) async-start(), calls=%async_computation.19 | async-start | bytes 2654208 | tf_op jit(solution)/shard_map/reduce_scatter | solution.py:150
  323.9 198.2 %reduce-scatter.14.cloned.1.call-start = ((), (), s32[]{:S(2)}) async-start(), calls=%async_computation.13 | async-start | bytes 2654208 | tf_op jit(solution)/shard_map/reduce_scatter | solution.py:147
  343.8 4.3 copy-start.14
  351.0 291.7 %reduce-scatter.26.cloned.1.call-start = ((), (), s32[]{:S(2)}) async-start(), calls=%async_computation.25 | async-start | bytes 7077888 | tf_op jit(solution)/shard_map/reduce_scatter | solution.py:155
  360.0 403.4 %reduce-scatter.24.cloned.1.call-start = ((), (), s32[]{:S(2)}) async-start(), calls=%async_computation.23 | async-start | bytes 7077888 | tf_op jit(solution)/shard_map/reduce_scatter | solution.py:154
  369.1 515.6 %reduce-scatter.22.cloned.1.call-start = ((), (), s32[]{:S(2)}) async-start(), calls=%async_computation.21 | async-start | bytes 7077888 | tf_op jit(solution)/shard_map/reduce_scatter | solution.py:153
  378.0 579.0 %reduce-scatter.18.cloned.1.call-start = ((), (), s32[]{:S(2)}) async-start(), calls=%async_computation.17 | async-start | bytes 2654208 | tf_op jit(solution)/shard_map/reduce_scatter | solution.py:149
  378.0 4.3 copy-start.15
  385.2 644.1 %reduce-scatter.16.cloned.1.call-start = ((), (), s32[]{:S(2)}) async-start(), calls=%async_computation.15 | async-start | bytes 2654208 | tf_op jit(solution)/shard_map/reduce_scatter | solution.py:148
  385.5 4.3 copy-start.16
  392.7 686.7 %all-reduce.10.cloned.1.call-start = ((), (), s32[]{:S(2)}) async-start(), calls=%async_computation.27 | async-start | bytes 3538944 | tf_op jit(solution)/shard_map/psum | solution.py:158
  644.6 438.5 %copy-start.30 = (u32[32]{0:T(128)S(1)}, u32[32]{0:T(128)}, u32[]{:S(2)}) copy-start(u32[32]{0:T(128)} %constant.37) | copy-start | bytes 388
  1030.9 120.5 %all-gather.20.cloned.1.call-start = ((), (), s32[]{:S(2)}) async-start(), calls=%async_computation.20 | async-start | bytes 1327104 | tf_op jit(solution)/shard_map/all_gather | solution.py:178
  1079.4 86.2 %all-gather.18.cloned.1.call-start = ((), (), s32[]{:S(2)}) async-start(), calls=%async_computation.18 | async-start | bytes 1327104 | tf_op jit(solution)/shard_map/all_gather | solution.py:175
  1080.0 127.7 %all-gather.16.cloned.1.call-start = ((), (), s32[]{:S(2)}) async-start(), calls=%async_computation.16 | async-start | bytes 1327104 | tf_op jit(solution)/shard_map/all_gather | solution.py:172
  1080.5 169.3 %all-gather.14.cloned.1.call-start = ((), (), s32[]{:S(2)}) async-start(), calls=%async_computation.14 | async-start | bytes 1327104 | tf_op jit(solution)/shard_map/all_gather | solution.py:169
  1081.1 230.2 %all-gather.26.cloned.1.call-start = ((), (), s32[]{:S(2)}) async-start(), calls=%async_computation.26 | async-start | bytes 3538944 | tf_op jit(solution)/shard_map/all_gather | solution.py:193
  1081.7 291.0 %all-gather.24.cloned.1.call-start = ((), (), s32[]{:S(2)}) async-start(), calls=%async_computation.24 | async-start | bytes 3538944 | tf_op jit(solution)/shard_map/all_gather | solution.py:190
  1082.3 352.0 %all-gather.22.cloned.1.call-start = ((), (), s32[]{:S(2)}) async-start(), calls=%async_computation.22 | async-start | bytes 3538944 | tf_op jit(solution)/shard_map/all_gather | solution.py:187
  1084.9 3.4 copy-start.6
  1084.9 4.0 copy-start.37
  1088.9 4.5 copy-start.13
  1088.9 4.5 copy-start.36
  1093.4 1.9 copy-start.8
  1093.4 2.2 copy-start.20
  1093.4 2.2 copy-start.23
  1095.6 3.8 copy-start.29
  1095.6 50.5 %copy-start.25 = (f32[1,2,4,128]{3,1,2,0:T(2,128)S(1)}, f32[1,2,4,128]{3,1,2,0:T(2,128)}, u32[]{:S(2)}) copy-start(f32[1,2,4,128]{3,1,2,0:T(2,128)} %copy-done.24) | copy-start | bytes 12292
  (9 other events, 10.7 us)
Sparse Core Ops, SparseCore 0:
  25.9 49.9 all-gather.11
  78.1 47.2 all-gather.9
  224.2 58.3 reduce-scatter.11
  318.7 58.0 reduce-scatter.9
  380.8 69.1 reduce-scatter.19
  453.9 68.0 reduce-scatter.13
  525.6 116.9 reduce-scatter.25
  646.2 117.0 reduce-scatter.23
  767.5 117.0 reduce-scatter.21
  888.6 68.3 reduce-scatter.17
  961.0 68.2 reduce-scatter.15
  1033.1 46.1 all-reduce.9
  1081.8 41.5 all-gather.19
  1125.7 39.8 all-gather.17
  1167.8 39.8 all-gather.15
  1210.0 39.8 all-gather.13
  1252.1 59.2 all-gather.25
  1313.6 59.0 all-gather.23
  1375.1 59.0 all-gather.21
where the time goes:
time: 1450 us
  waiting for transfers between devices  978 us (67%)
  matrix products  246 us (17%)
  other arithmetic  97.1 us (7%)
  local copies, waits for them, and re-layouts  57.2 us (4%)
  blocking collectives  51.3 us (4%)
  between operations  16.2 us (1%)
    reduce_scatter x1, waiting for transfers between devices, body(): lax.psum_scatter(d_gate_w, 'rows', scatter_dimension=0, tiled=True)  119 us
    reduce_scatter x1, waiting for transfers between devices, body(): lax.psum_scatter(d_down, 'rows', scatter_dimension=0, tiled=True)  119 us
    reduce_scatter x1, waiting for transfers between devices, body(): lax.psum_scatter(d_up_w, 'rows', scatter_dimension=0, tiled=True)  119 us
    reduce_scatter x1, waiting for transfers between devices, body(): lax.psum_scatter(d_key_w, 'rows', scatter_dimension=0, tiled=True)  70.7 us
    reduce_scatter x1, waiting for transfers between devices, body(): lax.psum_scatter(d_query_w, 'rows', scatter_dimension=0, tiled=True)  70.4 us
    reduce_scatter x1, waiting for transfers between devices, body(): lax.psum_scatter(d_value_w, 'rows', scatter_dimension=0, tiled=True)  70.4 us
    all_gather x1, waiting for transfers between devices, body(): lax.all_gather(grad_summed[8].astype(jnp.bfloat16), 'rows', axis=0, tiled...  58.7 us
    reduce_scatter x1, waiting for transfers between devices, body(): lax.psum_scatter(d_out_w, 'rows', scatter_dimension=0, tiled=True)  57.3 us
  transfers between devices with their start and end apart: 19, of which 16 were waited for; matrix products, arithmetic and copies ran while one was open for 19% of the time, Pallas kernels for 0%

commit v1 on v0

v1 whole, which is shorter than its diff:
```python
from functools import partial

import jax
import jax.numpy as jnp
from jax import lax
from jax.experimental import pallas as pl
from jax.experimental.pallas import tpu as pltpu
from jax.sharding import PartitionSpec as P

MESH = pl.DeviceIdType.MESH
HEAD_DIM = 64
EPSILON = 1e-06
MASKED = -1000000000.0
PIECE = 768
NT = 3
NC = 12


def flip(index, bit):
    unit = 1 << bit
    own = lax.rem(index // unit, 2)
    return own, index + (1 - 2 * own) * unit


class Links:
    def __init__(self, row_bits):
        seq, row = lax.axis_index("seq"), lax.axis_index("rows")
        self.core, other = flip(seq, 0)
        self.other_core = (other, row)
        x_bit, x_other = flip(seq, 1)
        dims = [(x_bit, (x_other, row))]
        for bit in range(row_bits):
            own, partner = flip(row, bit)
            dims.append((own, (seq, partner)))
        self.halving = dims[:3]
        self.extra = dims[3:]
        n = len(self.halving)
        orders = [(0, 1, 2), (1, 2, 0), (2, 0, 1)]
        self.orders = [[d for d in order if d < n] for order in orders]

    def all(self):
        return [self.other_core] + [p for _, p in self.halving + self.extra]


class Reducer:
    def __init__(self, links, grads, landing, small, send, recv, free):
        self.l, self.g, self.landing, self.small = links, grads, landing, small
        self.send, self.recv, self.free = send, recv, free
        n, e = len(links.halving), len(links.extra)
        self.n, self.e = n, e
        self.steps = 2 + 2 * n + e + 1

    def span(self, t, level):
        low = 0
        for k in range(level):
            low = low + self.l.halving[self.l.orders[t][k]][0] * (PIECE >> (k + 1))
        return low

    def copies(self, c, stage):
        l, n, e = self.l, self.n, self.e
        core = l.core
        if stage == 0:
            return [self.make(self.g.at[c, :, 1 - core], self.landing.at[c, :, pl.ds(0, PIECE)], c, stage, 0, l.other_core)]
        if stage <= n:
            out = []
            for t in range(NT):
                own, partner = l.halving[l.orders[t][stage - 1]]
                rows = PIECE >> stage
                low = pl.multiple_of(self.span(t, stage - 1) + (1 - own) * rows, 16)
                at = 2 * PIECE - 2 * rows
                out.append(self.make(self.g.at[c, t, core, pl.ds(low, rows)], self.landing.at[c, t, pl.ds(at, rows)], c, stage, t, partner))
            return out
        rows = PIECE >> n
        if stage <= n + e:
            partner = l.extra[stage - n - 1][1]
            out = []
            for t in range(NT):
                low = pl.multiple_of(self.span(t, n), 16)
                out.append(self.make(self.g.at[c, t, core, pl.ds(low, rows)], self.small.at[c, stage - n - 1, t], c, stage, t, partner))
            return out
        k = 2 * n + e + 1 - stage
        if k > 0:
            out = []
            for t in range(NT):
                partner = l.halving[l.orders[t][k - 1]][1]
                rows = PIECE >> k
                low = pl.multiple_of(self.span(t, k), 16)
                view = self.g.at[c, t, core, pl.ds(low, rows)]
                out.append(self.make(view, view, c, stage, t, partner))
            return out
        view = self.g.at[c, :, core]
        return [self.make(view, view, c, stage, 0, l.other_core)]

    def make(self, src, dst, c, stage, t, partner):
        return pltpu.make_async_remote_copy(
            src_ref=src, dst_ref=dst, send_sem=self.send.at[c, stage, t], recv_sem=self.recv.at[c, stage, t],
            device_id=partner, device_id_type=MESH)

    def fold(self, c, stage):
        n, e = self.n, self.e
        core = self.l.core
        if stage <= n:
            rows = PIECE >> stage
            at = 0 if stage == 0 else 2 * PIECE - 2 * rows
            for t in range(NT):
                low = pl.multiple_of(self.span(t, stage), 16)
                view = self.g.at[c, t, core, pl.ds(low, rows)]
                got = self.landing[c, t, pl.ds(at, rows)]
                view[...] = (view[...].astype(jnp.float32) + got.astype(jnp.float32)).astype(jnp.bfloat16)
        elif stage <= n + e:
            rows = PIECE >> n
            for t in range(NT):
                low = pl.multiple_of(self.span(t, n), 16)
                view = self.g.at[c, t, core, pl.ds(low, rows)]
                got = self.small[c, stage - n - 1, t]
                view[...] = (view[...].astype(jnp.float32) + got.astype(jnp.float32)).astype(jnp.bfloat16)

    def step(self, k, c):
        if k > 0:
            for copy in self.copies(c, k - 1):
                copy.wait()
            self.fold(c, k - 1)
            if k - 1 <= self.n:
                for t, partner in self.partners(k - 1):
                    pl.semaphore_signal(self.free.at[k - 1, t], inc=1, device_id=partner, device_id_type=MESH)
        if k < self.steps - 1:
            back = 2 * self.n + self.e + 1 - k
            if back <= self.n:
                for t, _ in self.partners(back):
                    pl.semaphore_wait(self.free.at[back, t], 1)
            for copy in self.copies(c, k):
                copy.start()

    def partners(self, level):
        if level == 0:
            return [(0, self.l.other_core)]
        return [(t, self.l.halving[self.l.orders[t][level - 1]][1]) for t in range(NT)]

    def round(self, r, finish):
        for k in reversed(range(self.steps)):
            c = r - k

            @pl.when((c >= 0) & (c < NC))
            def _():
                self.step(k, c)
                if k == self.steps - 1:
                    finish(c)


def scratch(row_bits):
    n, e = min(3, row_bits + 1), max(0, row_bits - 2)
    stages = 2 + 2 * n + e
    return [
        pltpu.VMEM((NC, NT, 2, PIECE, 128), jnp.bfloat16),
        pltpu.VMEM((NC, NT, 2 * PIECE - (PIECE >> n), 128), jnp.bfloat16),
        pltpu.VMEM((NC, max(e, 1), NT, PIECE >> n, 128), jnp.bfloat16),
        pltpu.SemaphoreType.DMA((NC, stages, NT)),
        pltpu.SemaphoreType.DMA((NC, stages, NT)),
        pltpu.SemaphoreType.REGULAR((n + 1, NT)),
    ]


def greet_row(count):
    seq, row = lax.axis_index("seq"), lax.axis_index("rows")
    barrier = pltpu.get_barrier_semaphore()
    for d in range(1, count):
        pl.semaphore_signal(barrier, inc=1, device_id=(lax.rem(seq + d, count), row), device_id_type=MESH)
    pl.semaphore_wait(barrier, count - 1)


def to_rows_kernel(count, blocks, ids, cotangent, x_out, ids_out, g_out, send, recv, own):
    seq, row = lax.axis_index("seq"), lax.axis_index("rows")
    greet_row(count)
    positions = blocks.shape[1]
    pairs = ((blocks, x_out, positions), (ids, ids_out, 8), (cotangent, g_out, positions))
    local, remote = [], []
    for a, (src, dst, size) in enumerate(pairs):
        mine = pl.ds(pl.multiple_of(seq * size, size), size)
        copy = pltpu.make_async_copy(src.at[seq], dst.at[mine], own.at[a])
        copy.start()
        local.append(copy)
        for d in range(1, count):
            peer = lax.rem(seq + d, count)
            copy = pltpu.make_async_remote_copy(
                src_ref=src.at[peer], dst_ref=dst.at[mine], send_sem=send.at[a, d], recv_sem=recv.at[a, d],
                device_id=(peer, row), device_id_type=MESH)
            copy.start()
            remote.append(copy)
    for copy in local + remote:
        copy.wait()


def to_rows(blocks, ids, cotangent):
    count, positions, features = blocks.shape
    anywhere = pl.BlockSpec(memory_space=pl.ANY)
    flat = jax.ShapeDtypeStruct((count * positions, features), blocks.dtype)
    wide = jnp.broadcast_to(ids[:, None, :], (count, 8, positions))
    return pl.pallas_call(
        partial(to_rows_kernel, count),
        out_shape=(flat, jax.ShapeDtypeStruct((count * 8, positions), ids.dtype), flat),
        in_specs=[anywhere] * 3, out_specs=[anywhere] * 3,
        scratch_shapes=[pltpu.SemaphoreType.DMA((3, count)), pltpu.SemaphoreType.DMA((3, count)), pltpu.SemaphoreType.DMA((3,))],
        compiler_params=pltpu.CompilerParams(collective_id=0, has_side_effects=True),
    )(blocks, wide, cotangent)


def sum_kernel(row_bits, count, src, y, dx, out, y_out, dx_out, grads, landing, small, send, recv, free, in_sem, out_sem, row_send, row_recv, own):
    links = Links(row_bits)
    seq, row = lax.axis_index("seq"), lax.axis_index("rows")
    reducer = Reducer(links, grads, landing, small, send, recv, free)
    barrier = pltpu.get_barrier_semaphore()
    for partner in links.all():
        pl.semaphore_signal(barrier, inc=1, device_id=partner, device_id_type=MESH)
    diagonal = (3 - seq, row)
    pl.semaphore_signal(barrier, inc=1, device_id=diagonal, device_id_type=MESH)
    pl.semaphore_wait(barrier, len(links.all()) + 1)

    def load(c):
        return pltpu.make_async_copy(src.at[c], grads.at[c], in_sem.at[c])

    def store(c):
        return pltpu.make_async_copy(grads.at[c], out.at[c], out_sem.at[c])

    for c in range(NC):
        load(c).start()
    moves = []
    positions = y.shape[0] // count
    for a, (a_src, a_dst) in enumerate(((y, y_out), (dx, dx_out))):
        copy = pltpu.make_async_copy(a_src.at[pl.ds(pl.multiple_of(seq * positions, positions), positions)], a_dst.at[seq], own.at[a])
        copy.start()
        moves.append(copy)
        for d in range(1, count):
            peer = lax.rem(seq + d, count)
            copy = pltpu.make_async_remote_copy(
                src_ref=a_src.at[pl.ds(pl.multiple_of(peer * positions, positions), positions)], dst_ref=a_dst.at[seq],
                send_sem=row_send.at[a, d], recv_sem=row_recv.at[a, d], device_id=(peer, row), device_id_type=MESH)
            copy.start()
            moves.append(copy)

    def body(r, _):
        @pl.when(r < NC)
        def _():
            load(r).wait()

        reducer.round(r, lambda c: store(c).start())
        return 0

    lax.fori_loop(0, NC + reducer.steps - 1, body, 0)
    for c in range(NC):
        store(c).wait()
    for copy in moves:
        copy.wait()


def sum_all(grads, y, dx, row_bits, count):
    anywhere = pl.BlockSpec(memory_space=pl.ANY)
    shape = (count, y.shape[0] // count, y.shape[1])
    back = jax.ShapeDtypeStruct(shape, y.dtype)
    return pl.pallas_call(
        partial(sum_kernel, row_bits, count),
        out_shape=(jax.ShapeDtypeStruct(grads.shape, grads.dtype), back, back),
        in_specs=[anywhere] * 3, out_specs=[anywhere] * 3,
        scratch_shapes=scratch(row_bits) + [pltpu.SemaphoreType.DMA((NC,)), pltpu.SemaphoreType.DMA((NC,)),
            pltpu.SemaphoreType.DMA((2, count)), pltpu.SemaphoreType.DMA((2, count)), pltpu.SemaphoreType.DMA((2,))],
        compiler_params=pltpu.CompilerParams(collective_id=1, has_side_effects=True, vmem_limit_bytes=60 * 2**20),
    )(grads, y, dx)


def rms_norm(value, gain):
    return value * lax.rsqrt(jnp.mean(value * value, axis=-1, keepdims=True) + EPSILON) * gain


def outer_sum(left, right):
    return lax.dot_general(left, right, (((0,), (0,)), ((), ())), preferred_element_type=jnp.float32)


def back_project(gradient, weight):
    return lax.dot_general(gradient, weight, (((1,), (1,)), ((), ())), preferred_element_type=jnp.float32)


def halves(piece):
    return piece.reshape(PIECE, 2, 128).transpose(1, 0, 2).astype(jnp.bfloat16)


def whole(pair):
    return pair.transpose(1, 0, 2).reshape(PIECE, 256)


def body(row_bits, blocks, segment_ids, cotangent, w_query, w_key, w_value, w_out, norm_one, norm_two, w_gate, w_up, w_down):
    count, positions, features = blocks.shape
    x_low, ids, grad_low = to_rows(blocks, segment_ids, cotangent)
    ids = ids.reshape(count, 8, positions)[:, 0, :].reshape(-1)
    tokens = x_low.shape[0]
    heads = features // HEAD_DIM
    x_flat = x_low.astype(jnp.float32)
    normed_one = rms_norm(x_flat, norm_one).astype(jnp.bfloat16)

    def project(weight):
        made = jnp.dot(normed_one, weight, preferred_element_type=jnp.float32)
        return made.astype(jnp.bfloat16).reshape(tokens, heads, HEAD_DIM)

    query, key, value = project(w_query), project(w_key), project(w_value)
    same_doc = ids[:, None] == ids[None, :]
    scores = jnp.einsum("qhd,khd->hqk", query, key, preferred_element_type=jnp.float32) * HEAD_DIM ** (-0.5)
    scores = jnp.where(same_doc, scores, MASKED)
    exponent = jnp.exp(scores - jnp.max(scores, axis=-1, keepdims=True))
    probability = (exponent / jnp.sum(exponent, axis=-1, keepdims=True)).astype(jnp.bfloat16)
    mixed = jnp.einsum("hqk,khd->qhd", probability, value, preferred_element_type=jnp.float32)
    mixed = mixed.astype(jnp.bfloat16).reshape(tokens, features)
    x_one = x_flat + jnp.dot(mixed, w_out, preferred_element_type=jnp.float32)
    normed_two = rms_norm(x_one, norm_two).astype(jnp.bfloat16)
    gate_value = jnp.dot(normed_two, w_gate, preferred_element_type=jnp.float32)
    up_value = jnp.dot(normed_two, w_up, preferred_element_type=jnp.float32)
    activated, gelu_back = jax.vjp(partial(jax.nn.gelu, approximate=True), gate_value)
    hidden = (activated * up_value).astype(jnp.bfloat16)
    result = (x_one + jnp.dot(hidden, w_down, preferred_element_type=jnp.float32)).astype(jnp.bfloat16)
    gradient = grad_low.astype(jnp.float32)
    d_down = outer_sum(hidden, grad_low)
    d_hidden = back_project(grad_low, w_down)
    d_gate = gelu_back(d_hidden * up_value)[0].astype(jnp.bfloat16)
    d_up = (d_hidden * activated).astype(jnp.bfloat16)
    d_gate_w = outer_sum(normed_two, d_gate)
    d_up_w = outer_sum(normed_two, d_up)
    d_normed_two = back_project(d_gate, w_gate) + back_project(d_up, w_up)
    d_x_part, d_norm_two = jax.vjp(rms_norm, x_one, norm_two)[1](d_normed_two)
    d_x_one = gradient + d_x_part
    d_branch = d_x_one.astype(jnp.bfloat16)
    d_out_w = outer_sum(mixed, d_branch)
    d_mixed = back_project(d_branch, w_out).astype(jnp.bfloat16).reshape(tokens, heads, HEAD_DIM)
    d_probs = jnp.einsum("qhd,khd->hqk", d_mixed, value, preferred_element_type=jnp.float32)
    wide = probability.astype(jnp.float32)
    d_scores = (wide * (d_probs - jnp.sum(wide * d_probs, axis=-1, keepdims=True))).astype(jnp.bfloat16)
    scale = HEAD_DIM ** (-0.5)
    d_query = jnp.einsum("hqk,khd->qhd", d_scores, key, preferred_element_type=jnp.float32) * scale
    d_key = jnp.einsum("hqk,qhd->khd", d_scores, query, preferred_element_type=jnp.float32) * scale
    d_value = jnp.einsum("hqk,qhd->khd", probability, d_mixed, preferred_element_type=jnp.float32)
    d_query, d_key, d_value = (d.astype(jnp.bfloat16).reshape(tokens, features) for d in (d_query, d_key, d_value))
    d_normed_one = back_project(d_query, w_query) + back_project(d_key, w_key) + back_project(d_value, w_value)
    d_x_first, d_norm_one = jax.vjp(rms_norm, x_flat, norm_one)[1](d_normed_one)
    d_input = (d_x_one + d_x_first).astype(jnp.bfloat16)
    d_qkv = [outer_sum(normed_one, d) for d in (d_query, d_key, d_value)]
    pieces = []
    for c in range(8):
        cols = slice(256 * c, 256 * c + 256)
        down = jnp.concatenate([d_down[cols, 256 * j : 256 * j + 256] for j in range(3)])
        pieces += [d_gate_w[:, cols], d_up_w[:, cols], down]
    pieces += [d_out_w[:, 256 * j : 256 * j + 256] for j in range(3)]
    for j in range(3):
        pieces += [d[:, 256 * j : 256 * j + 256] for d in d_qkv]
    stacked = jnp.stack([halves(p) for p in pieces]).reshape(NC, NT, 2, PIECE, 128)
    summed, y_back, dx_back = sum_all(stacked, result, d_input, row_bits, count)
    gains = lax.psum(jnp.stack([d_norm_one, d_norm_two]), ("seq", "rows"))
    summed = summed.astype(jnp.float32)
    parts = [[whole(summed[c, t]) for t in range(NT)] for c in range(NC)]
    g_gate = jnp.concatenate([parts[c][0] for c in range(8)], axis=1)
    g_up = jnp.concatenate([parts[c][1] for c in range(8)], axis=1)
    g_down = jnp.concatenate([parts[c][2].reshape(3, 256, 256).transpose(1, 0, 2).reshape(256, 768) for c in range(8)], axis=0)
    g_out = jnp.concatenate(parts[8], axis=1)
    g_q, g_k, g_v = (jnp.concatenate([parts[9 + j][t] for j in range(3)], axis=1) for t in range(NT))
    return (y_back, dx_back, g_q, g_k, g_v, g_out, gains[0], gains[1], g_gate, g_up, g_down)


def solution(mesh):
    split = P("rows", "seq", None)
    row_bits = (mesh.shape["rows"] - 1).bit_length()
    return jax.shard_map(
        partial(body, row_bits),
        mesh=mesh,
        in_specs=(split, P("rows", "seq"), split) + (P(),) * 9,
        out_specs=(split, split) + (P(),) * 9,
        check_vma=False,
    )
```

time: 1450 us -> 794 us (0.55)
  waiting for transfers between devices: 978 us -> 0 us
  Pallas kernels: 0 us -> 201 us
  local copies, waits for them, and re-layouts: 57.2 us -> 253 us
  matrix products: 246 us -> 188 us
    reduce_scatter x9 -> x0, waiting for transfers between devices: 626 us -> none  [the longest x1 119 us: body(): lax.psum_scatter(d_gate_w, 'rows', scatter_dimension=0, tiled=True)]
    all_gather x9 -> x0, waiting for transfers between devices: 300 us -> none  [the longest x1 58.7 us: body(): lax.all_gather(grad_summed[8].astype(jnp.bfloat16), 'rows', axis=0, tiled...]
    pallas_call x0 -> x2, Pallas kernels: none -> 201 us  [the longest x1 163 us: sum_all(): pl.pallas_call(partial(sum_kernel, row_bits, count), out_shape=(jax.Shape...]
    transpose x0 -> x46, local copies, waits for them, and re-layouts: none -> 104 us  [the longest x38 91.5 us: whole(): return pair.transpose(1, 0, 2).reshape(PIECE, 256)]
    unnamed x88 -> x231, local copies, waits for them, and re-layouts: 14.1 us -> 103 us
    psum x1 -> x0, waiting for transfers between devices: 48.4 us -> none  [body(): lax.psum(grad_shares[0].astype(jnp.bfloat16), 'seq').astype(jnp.float32)]
    unnamed x2 -> x0, blocking collectives: 39.3 us -> none
    psum x1, blocking collectives: 5.64 us -> 40 us  [body(): gains = lax.psum(jnp.stack([d_norm_one, d_norm_two]), ('seq', 'rows'))]
  transfers between devices with their start and end apart: 19 -> 0, of which waited for: 16 -> 0; matrix products, arithmetic and copies ran while one was open for 19% -> 0% of each run, Pallas kernels for 0% -> 0%
where the time goes in v1:
time: 794 us; the launch traced here: 787 us
  local copies, waits for them, and re-layouts  253 us (32%)
  Pallas kernels  201 us (25%)
  matrix products  188 us (24%)
  other arithmetic  104 us (13%)
  blocking collectives  40 us (5%)
    pallas_call x1, Pallas kernels, sum_all(): pl.pallas_call(partial(sum_kernel, row_bits, count), out_shape=(jax.Shape...  163 us
    unnamed x231, local copies, waits for them, and re-layouts  103 us
    transpose x38, local copies, waits for them, and re-layouts, whole(): return pair.transpose(1, 0, 2).reshape(PIECE, 256)  91.5 us
    convert_element_type x1, other arithmetic, body(): (wide * (d_probs - jnp.sum(wide * d_probs, axis=-1, keepdims=True))).asty...  40.9 us
    psum x1, blocking collectives, body(): gains = lax.psum(jnp.stack([d_norm_one, d_norm_two]), ('seq', 'rows'))  40 us
    pallas_call x1, Pallas kernels, to_rows(): pl.pallas_call(partial(to_rows_kernel, count), out_shape=(flat, jax.Shape...  38.1 us
    convert_element_type x1, other arithmetic, body(): (exponent / jnp.sum(exponent, axis=-1, keepdims=True)).astype(jnp.bfloat16)  26.5 us
    sub x1, matrix products, body(): exponent = jnp.exp(scores - jnp.max(scores, axis=-1, keepdims=True))  25.7 us

profile of v1, /device:TPU:0, one launch (start us, length us, event | category | flops | bytes accessed | tf_op | source)
XLA Modules:
  0.0 786.6 jit_solution(17522030375994779658)
XLA Ops:
  2.1 38.1 %shard_map.203 = (bf16[1024,768]{1,0:T(8,128)(2,1)}, s32[32,256]{1,0:T(8,128)}, bf16[1024,768]{1,0:T(8,128)(2,1)}) custom-call(bf16[4,256,768]{2,1,0:T(8,128)(2,1)} %blocks.1, s32[4,8,256]{2,1,0:T(8,128)} %broadcast_in_dim.14.ids, bf16[4,256,768]{2,1,0:T(8,128)(2,1)} %cotangent.1), custom_call_target="tpu_custom_call" | custom-call | tf_op jit(solution)/shard_map/pallas_call | solution.py:198
  45.0 4.6 convolution_convert_fusion.7
  49.6 2.8 convolution_convert_fusion.6
  52.4 2.8 convolution_convert_fusion.8
  55.2 5.8 fusion.68
  61.0 25.7 %fusion.67 = (f32[12,1024]{1,0:T(8,128)S(1)}, f32[12,1024,1024]{1,2,0:T(8,128)}) fusion(pred[1024,1024]{0,1:T(8,128)(4,1)} %broadcast_compare_fusion, bf16[1024,12,64]{0,2,1:T(8,128)(2,1)} %bitcast.653, bf16[1024,12,64]{0,2,1:T(8,128)(2,1)} %bitcast.657), kind=kOutput, calls=%fused_computation.231 | convolution fusion | flops 1660945408 | bytes 54575104 | tf_op jit(solution)/shard_map/sub | solution.py:306
  86.6 26.5 %divide_convert_fusion = bf16[12,1024,1024]{1,2,0:T(8,128)(2,1)} fusion(f32[12,1024,1024]{1,2,0:T(8,128)} %get-tuple-element.132, f32[12,1024]{1,0:T(8,128)S(1)} %get-tuple-element.131), kind=kLoop, calls=%fused_computation.5 | loop fusion | flops 25165824 | bytes 75546624 | tf_op jit(solution)/shard_map/convert_element_type | solution.py:307
  113.1 13.3 %convolution_convert_fusion.5 = bf16[12,64,1024]{2,1,0:T(8,128)(2,1)S(1)} fusion(bf16[1024,12,64]{0,2,1:T(8,128)(2,1)} %bitcast.607, bf16[12,1024,1024]{1,2,0:T(8,128)(2,1)} %divide_convert_fusion), kind=kOutput, calls=%fused_computation.60 | convolution fusion | flops 1611399168 | bytes 28311552 | tf_op jit(solution)/shard_map/hqk,khd->qhd/dot_general | solution.py:308
  130.0 5.6 fusion.69
  135.6 15.7 %multiply_convert_fusion = (bf16[1024,2048]{1,0:T(8,128)(2,1)}, bf16[1024,2048]{1,0:T(8,128)(2,1)}, bf16[1024,2048]{1,0:T(8,128)(2,1)}) fusion(f32[1024,2048]{1,0:T(8,128)} %fusion.69, f32[1024,2048]{1,0:T(8,128)} %fusion.68, bf16[1024,768]{1,0:T(8,128)(2,1)S(1)} %multiply_convert_fusion.4, bf16[768,2048]{1,0:T(8,128)(2,1)S(1)} %copy-done), kind=kOutput, calls=%fused_computation.21 | convolution fusion | flops 3275751424 | bytes 34078720 | tf_op jit(solution)/shard_map/dot_general | solution.py:313
  151.3 6.9 add_convert_fusion.y
  158.3 3.8 convolution_convert_fusion
  166.5 3.5 fusion.70
  170.0 3.9 convolution_convert_fusion.2
  177.2 4.0 multiply_reduce_fusion
  181.3 3.7 convolution_convert_fusion.1
  194.9 3.8 convolution_convert_fusion.4
  198.7 13.3 %convolution_convert_fusion.3 = bf16[12,64,1024]{2,1,0:T(8,128)(2,1)S(1)} fusion(bf16[1024,12,64]{0,2,1:T(8,128)(2,1)} %bitcast.603, bf16[12,1024,1024]{1,2,0:T(8,128)(2,1)} %divide_convert_fusion), kind=kOutput, calls=%fused_computation.58 | convolution fusion | flops 1611399168 | bytes 28311552 | tf_op jit(solution)/shard_map/hqk,qhd->khd/dot_general | solution.py:336
  246.5 25.4 %fusion.1 = (f32[12,1024]{1,0:T(8,128)}, f32[12,1024,1024]{1,2,0:T(8,128)}) fusion(bf16[12,1024,1024]{1,2,0:T(8,128)(2,1)} %divide_convert_fusion, bf16[1024,12,64]{0,2,1:T(8,128)(2,1)S(1)} %bitcast.604, bf16[1024,12,64]{0,2,1:T(8,128)(2,1)S(1)} %bitcast.608), kind=kOutput, calls=%fused_computation.3 | convolution fusion | flops 1648349184 | bytes 78692352 | tf_op jit(solution)/shard_map/qhd,khd->hqk/dot_general | solution.py:330
  271.9 40.9 %fusion.2 = bf16[12,1024,1024]{1,2,0:T(8,128)(2,1)} fusion(f32[12,1024,1024]{1,2,0:T(8,128)} %get-tuple-element.137, f32[12,1024]{1,0:T(8,128)} %get-tuple-element.136, f32[12,1024,1024]{1,2,0:T(8,128)} %get-tuple-element.132, f32[12,1024]{1,0:T(8,128)} %copy-done.64), kind=kLoop, calls=%fused_computation.4 | loop fusion | flops 75497472 | bytes 125927424 | tf_op jit(solution)/shard_map/convert_element_type | solution.py:332
  312.8 14.0 %multiply_convert_fusion.2 = bf16[12,64,1024]{2,1,0:T(8,128)(2,1)} fusion(bf16[1024,12,64]{0,2,1:T(8,128)(2,1)S(1)} %bitcast.654, bf16[12,1024,1024]{1,2,0:T(8,128)(2,1)} %fusion.2), kind=kOutput, calls=%fused_computation.47 | convolution fusion | flops 1612185600 | bytes 28311552 | tf_op jit(solution)/shard_map/hqk,qhd->khd/dot_general | solution.py:335
  326.9 14.4 %multiply_convert_fusion.3 = bf16[12,64,1024]{2,1,0:T(8,128)(2,1)} fusion(bf16[1024,12,64]{0,2,1:T(8,128)(2,1)} %bitcast.658, bf16[12,1024,1024]{1,2,0:T(8,128)(2,1)} %fusion.2), kind=kOutput, calls=%fused_computation.48 | convolution fusion | flops 1612185600 | bytes 28311552 | tf_op jit(solution)/shard_map/hqk,khd->qhd/dot_general | solution.py:334
  372.6 4.0 fusion.19
  376.6 40.0 %psum.7 = f32[2,768]{1,0:T(2,128)S(1)} all-reduce(f32[2,768]{1,0:T(2,128)S(1)} %pad_maximum_fusion.4), channel_id=1, replica_groups=mesh['seq'=4,'rows'=8] {'seq','rows'}, use_global_device_ids=true, to_apply=%region_9.10 | all-reduce | flops 1536 | bytes 12288 | tf_op jit(solution)/shard_map/psum | solution.py:352
  416.6 4.8 fusion.22.dx
  421.4 162.5 %shard_map.204 = (bf16[12,3,2,768,128]{4,3,2,1,0:T(8,128)(2,1)}, bf16[4,256,768]{2,1,0:T(8,128)(2,1)}, bf16[4,256,768]{2,1,0:T(8,128)(2,1)}) custom-call(bf16[12,3,2,768,128]{4,3,2,1,0:T(8,128)(2,1)} %bitcast.99.src, bf16[1024,768]{1,0:T(8,128)(2,1)} %add_convert_fusion.y, bf16[1024,768]{1,0:T(8,128)(2,1)} %fusion.22.dx), custom_call_target="tpu_custom_call" | custom-call | tf_op jit(solution)/shard_map/pallas_call | solution.py:259
  584.6 16.0 %convert_element_type.427 = f32[12,3,2,768,128]{4,3,2,1,0:T(8,128)} convert(bf16[12,3,2,768,128]{4,3,2,1,0:T(8,128)(2,1)} %get-tuple-element.22) | non-fusion elementwise | flops 7077888 | bytes 42467328 | tf_op jit(solution)/shard_map/convert_element_type | solution.py:353
  600.6 8.9 %slice_bitcast_fusion.19 = (f32[768,2,128]{2,0,1:T(8,128)}, f32[768,2,128]{2,0,1:T(8,128)}, f32[768,2,128]{2,0,1:T(8,128)}, f32[768,2,128]{2,0,1:T(8,128)}, f32[...) fusion(f32[12,3,2,768,128]{4,3,2,1,0:T(8,128)} %convert_element, ...), kind=kLoop, calls=%fused_computation.87 | loop fusion | bytes 26738688 | tf_op jit(solution)/shard_map/transpose | solution.py:286
  609.4 10.5 %slice_bitcast_fusion = (f32[768,2,128]{2,0,1:T(8,128)}, f32[768,2,128]{2,0,1:T(8,128)}, f32[768,2,128]{2,0,1:T(8,128)}, f32[768,2,128]{2,0,1:T(8,128)}, f32[768...) fusion(f32[12,3,2,768,128]{4,3,2,1,0:T(8,128)} %convert_element, ...), kind=kLoop, calls=%fused_computation.68 | loop fusion | bytes 29884416 | tf_op jit(solution)/shard_map/transpose | solution.py:286
  620.0 2.7 copy.147
  622.6 2.6 reshape_reshape.31
  625.3 2.3 copy.148
  629.9 2.4 copy.120
  632.2 2.3 copy.119
  646.3 2.4 copy.113
  655.8 2.4 copy.110
  693.1 2.6 copy.135
  695.7 2.6 reshape_reshape.25
  700.7 2.6 copy.133
  703.3 2.6 reshape_reshape.24
  717.4 2.3 copy.128
  719.7 2.3 copy.127
  722.0 2.5 copy.126
  726.8 2.3 copy.124
  743.7 6.6 copy.154
  760.0 6.6 copy.155
  775.5 6.7 copy.153
  782.2 2.8 copy.267
  (315 shorter events, 200.1 us)
Async XLA Ops:
  0.6 135.0 %copy-start = (bf16[768,2048]{1,0:T(8,128)(2,1)S(1)}, bf16[768,2048]{1,0:T(8,128)(2,1)}, u32[]{:S(2)}) copy-start(bf16[768,2048]{1,0:T(8,128)(2,1)} %param.22) | copy-start | bytes 9437188
  0.7 44.3 %copy-start.69 = (f32[768]{0:T(1024)S(1)}, f32[768]{0:T(1024)}, u32[]{:S(2)}) copy-start(f32[768]{0:T(1024)} %param.19) | copy-start | bytes 9220
  43.4 9.0 %copy-start.65 = (f32[1024]{0:T(1024)}, f32[1024]{0:T(1024)S(1)}, u32[]{:S(2)}) copy-start(f32[1024]{0:T(1024)S(1)} %fusion.51) | copy-start | bytes 12292
  86.6 26.5 %copy-start.64 = (f32[12,1024]{1,0:T(8,128)}, f32[12,1024]{1,0:T(8,128)S(1)}, u32[]{:S(2)}) copy-start(f32[12,1024]{1,0:T(8,128)S(1)} %get-tuple-element.131) | copy-start | bytes 147460
  113.1 13.3 %copy-start.3 = (bf16[1024,768]{1,0:T(8,128)(2,1)S(1)}, bf16[1024,768]{1,0:T(8,128)(2,1)}, u32[]{:S(2)}) copy-start(bf16[1024,768]{1,0:T(8,128)(2,1)} %get-tuple-element.17) | copy-start | bytes 4718596
  113.1 13.3 %copy-start.75 = (bf16[768,768]{1,0:T(8,128)(2,1)S(1)}, bf16[768,768]{1,0:T(8,128)(2,1)}, u32[]{:S(2)}) copy-start(bf16[768,768]{1,0:T(8,128)(2,1)} %param.18) | copy-start | bytes 3538948
  135.6 15.7 %copy-start.73 = (bf16[2048,768]{1,0:T(8,128)(2,1)S(1)}, bf16[2048,768]{1,0:T(8,128)(2,1)}, u32[]{:S(2)}) copy-start(bf16[2048,768]{1,0:T(8,128)(2,1)} %param.23) | copy-start | bytes 9437188
  151.3 7.0 copy-start.61
  151.3 6.9 copy-start.81
  185.9 9.0 %copy-start.5 = (f32[1024,768]{1,0:T(8,128)}, f32[1024,768]{1,0:T(8,128)S(1)}, u32[]{:S(2)}) copy-start(f32[1024,768]{1,0:T(8,128)S(1)} %fusion.20) | copy-start | bytes 9437188
  198.7 13.3 %copy-start.4 = (bf16[1024,768]{1,0:T(8,128)(2,1)S(1)}, bf16[1024,768]{1,0:T(8,128)(2,1)}, u32[]{:S(2)}) copy-start(bf16[1024,768]{1,0:T(8,128)(2,1)} %get-tuple-element.17) | copy-start | bytes 4718596
  198.7 13.3 %copy-start.66 = (f32[1024]{0:T(1024)S(1)}, f32[1024]{0:T(1024)}, u32[]{:S(2)}) copy-start(f32[1024]{0:T(1024)} %copy-done.65) | copy-start | bytes 12292
  198.7 13.3 %copy-start.70 = (f32[768]{0:T(1024)S(1)}, f32[768]{0:T(1024)}, u32[]{:S(2)}) copy-start(f32[768]{0:T(1024)} %param.19) | copy-start | bytes 9220
  214.6 10.8 %copy-start.47 = (bf16[96,2,8,128]{3,2,1,0:T(8,128)(2,1)S(1)}, bf16[96,2,8,128]{3,2,1,0:T(8,128)(2,1)}, u32[]{:S(2)}) copy-start(bf16[96,2,8,128]{3,2,1,0:T(8,128)(2,1)} %get-tuple-element.112) | copy-start | bytes 1179652
  215.9 14.1 %copy-start.45 = (bf16[96,2,8,128]{3,2,1,0:T(8,128)(2,1)S(1)}, bf16[96,2,8,128]{3,2,1,0:T(8,128)(2,1)}, u32[]{:S(2)}) copy-start(bf16[96,2,8,128]{3,2,1,0:T(8,128)(2,1)} %get-tuple-element.111) | copy-start | bytes 1179652
  217.9 12.9 %copy-start.50 = (bf16[96,2,8,128]{3,2,1,0:T(8,128)(2,1)S(1)}, bf16[96,2,8,128]{3,2,1,0:T(8,128)(2,1)}, u32[]{:S(2)}) copy-start(bf16[96,2,8,128]{3,2,1,0:T(8,128)(2,1)} %get-tuple-element.103) | copy-start | bytes 1179652
  219.9 11.7 %copy-start.59 = (bf16[96,2,8,128]{3,2,1,0:T(8,128)(2,1)S(1)}, bf16[96,2,8,128]{3,2,1,0:T(8,128)(2,1)}, u32[]{:S(2)}) copy-start(bf16[96,2,8,128]{3,2,1,0:T(8,128)(2,1)} %get-tuple-element.141) | copy-start | bytes 1179652
  221.7 10.7 %copy-start.41 = (bf16[96,2,8,128]{3,2,1,0:T(8,128)(2,1)S(1)}, bf16[96,2,8,128]{3,2,1,0:T(8,128)(2,1)}, u32[]{:S(2)}) copy-start(bf16[96,2,8,128]{3,2,1,0:T(8,128)(2,1)} %get-tuple-element.110) | copy-start | bytes 1179652
  223.6 9.6 %copy-start.49 = (bf16[96,2,8,128]{3,2,1,0:T(8,128)(2,1)S(1)}, bf16[96,2,8,128]{3,2,1,0:T(8,128)(2,1)}, u32[]{:S(2)}) copy-start(bf16[96,2,8,128]{3,2,1,0:T(8,128)(2,1)} %get-tuple-element.102) | copy-start | bytes 1179652
  225.5 8.5 %copy-start.58 = (bf16[96,2,8,128]{3,2,1,0:T(8,128)(2,1)S(1)}, bf16[96,2,8,128]{3,2,1,0:T(8,128)(2,1)}, u32[]{:S(2)}) copy-start(bf16[96,2,8,128]{3,2,1,0:T(8,128)(2,1)} %get-tuple-element.142) | copy-start | bytes 1179652
  226.2 8.5 %copy-start.38 = (bf16[96,2,8,128]{3,2,1,0:T(8,128)(2,1)S(1)}, bf16[96,2,8,128]{3,2,1,0:T(8,128)(2,1)}, u32[]{:S(2)}) copy-start(bf16[96,2,8,128]{3,2,1,0:T(8,128)(2,1)} %get-tuple-element.109) | copy-start | bytes 1179652
  228.1 7.4 copy-start.48
  230.0 6.3 copy-start.57
  230.8 6.3 copy-start.37
  231.6 6.3 copy-start.46
  232.4 6.3 copy-start.56
  233.2 6.3 copy-start.36
  234.0 6.3 copy-start.44
  234.8 6.3 copy-start.55
  235.6 6.3 copy-start.35
  236.3 6.3 copy-start.40
  237.1 6.3 copy-start.54
  237.9 6.3 copy-start.43
  238.7 6.2 copy-start.42
  240.3 6.2 copy-start.6
  240.3 6.2 copy-start.9
  271.9 40.9 %copy-start.29 = (bf16[1024,768]{0,1:T(8,128)(2,1)S(1)}, bf16[1024,768]{0,1:T(8,128)(2,1)}, u32[]{:S(2)}) copy-start(bf16[1024,768]{0,1:T(8,128)(2,1)} %convolution_convert_fusion.7) | copy-start | bytes 4718596
  326.9 14.4 %copy-start.30 = (bf16[12,64,1024]{2,1,0:T(8,128)(2,1)S(1)}, bf16[12,64,1024]{2,1,0:T(8,128)(2,1)}, u32[]{:S(2)}) copy-start(bf16[12,64,1024]{2,1,0:T(8,128)(2,1)} %multiply_convert_fusion.2) | copy-start | bytes 4718596
  342.8 6.8 copy-start.32
  357.9 7.3 copy-start.52
  357.9 8.1 %copy-start.34 = (bf16[768,2,128]{2,0,1:T(8,128)(2,1)S(1)}, bf16[768,2,128]{2,0,1:T(8,128)(2,1)}, u32[]{:S(2)}) copy-start(bf16[768,2,128]{2,0,1:T(8,128)(2,1)} %copy.101) | copy-start | bytes 1179652
  357.9 8.9 %copy-start.53 = (bf16[768,2,128]{2,0,1:T(8,128)(2,1)S(1)}, bf16[768,2,128]{2,0,1:T(8,128)(2,1)}, u32[]{:S(2)}) copy-start(bf16[768,2,128]{2,0,1:T(8,128)(2,1)} %copy.102) | copy-start | bytes 1179652
  357.9 9.7 %copy-start.51 = (bf16[768,2,128]{2,0,1:T(8,128)(2,1)S(1)}, bf16[768,2,128]{2,0,1:T(8,128)(2,1)}, u32[]{:S(2)}) copy-start(bf16[768,2,128]{2,0,1:T(8,128)(2,1)} %copy.103) | copy-start | bytes 1179652
  359.8 9.3 %copy-start.76 = (bf16[768,768]{1,0:T(8,128)(2,1)S(1)}, bf16[768,768]{1,0:T(8,128)(2,1)}, u32[]{:S(2)}) copy-start(bf16[768,768]{1,0:T(8,128)(2,1)} %param.15) | copy-start | bytes 3538948
  372.6 44.0 %copy-start.68 = (f32[1024]{0:T(1024)S(1)}, f32[1024]{0:T(1024)}, u32[]{:S(2)}) copy-start(f32[1024]{0:T(1024)} %copy-done.67) | copy-start | bytes 12292
  733.7 6.2 copy-start.24
  760.0 8.9 %copy-start.16 = (f32[768,2,128]{0,2,1:T(8,128)S(1)}, f32[768,2,128]{0,2,1:T(8,128)}, u32[]{:S(2)}) copy-start(f32[768,2,128]{0,2,1:T(8,128)} %copy.118) | copy-start | bytes 2359300
  775.5 10.6 %copy-start.1 = (bf16[768,2048]{1,0:T(8,128)(2,1)S(1)}, bf16[768,2048]{1,0:T(8,128)(2,1)}, u32[]{:S(2)}) copy-start(bf16[768,2048]{1,0:T(8,128)(2,1)} %param.22) | copy-start | bytes 9437188
  (34 other events, 115.2 us)

commit v2 on v1

v2 whole, which is shorter than its diff:
```python
from functools import partial

import jax
import jax.numpy as jnp
from jax import lax
from jax.experimental import pallas as pl
from jax.experimental.pallas import tpu as pltpu
from jax.sharding import PartitionSpec as P

MESH = pl.DeviceIdType.MESH
HEAD_DIM = 64
EPSILON = 1e-06
MASKED = -1000000000.0
PIECE = 768
NT = 3
COLS = 256
SLOTS = 3
BF = jnp.bfloat16
F32 = jnp.float32
NN = (((1,), (0,)), ((), ()))
NTRANS = (((1,), (1,)), ((), ()))


def dot(left, right, dims=NN):
    return lax.dot_general(left, right, dims, preferred_element_type=F32)


def flip(index, bit):
    unit = 1 << bit
    own = lax.rem(index // unit, 2)
    return own, index + (1 - 2 * own) * unit


class Links:
    def __init__(self, row_bits):
        seq, row = lax.axis_index("seq"), lax.axis_index("rows")
        self.seq, self.row = seq, row
        self.core, other = flip(seq, 0)
        self.other_core = (other, row)
        x_bit, x_other = flip(seq, 1)
        diagonal = flip(other, 1)[1]
        self.peers = [seq, other, x_other, diagonal]
        dims = [(x_bit, (x_other, row))]
        for bit in range(row_bits):
            own, partner = flip(row, bit)
            dims.append((own, (seq, partner)))
        self.halving = dims[:3]
        self.extra = dims[3:]
        n = len(self.halving)
        orders = [(0, 1, 2), (1, 2, 0), (2, 0, 1)]
        self.orders = [[d for d in order if d < n] for order in orders]

    def all(self):
        return [self.other_core] + [p for _, p in self.halving + self.extra]

    def greet(self):
        barrier = pltpu.get_barrier_semaphore()
        whom = self.all() + [(self.peers[3], self.row)]
        for partner in whom:
            pl.semaphore_signal(barrier, inc=1, device_id=partner, device_id_type=MESH)
        pl.semaphore_wait(barrier, len(whom))


class Reducer:
    def __init__(self, links, grads, landing, small, send, recv, free):
        self.l, self.g, self.landing, self.small = links, grads, landing, small
        self.send, self.recv, self.free = send, recv, free
        n, e = len(links.halving), len(links.extra)
        self.n, self.e = n, e
        self.steps = 2 + 2 * n + e + 1

    def span(self, t, level):
        low = 0
        for k in range(level):
            low = low + self.l.halving[self.l.orders[t][k]][0] * (PIECE >> (k + 1))
        return low if level == 0 else pl.multiple_of(low, 16)

    def copies(self, c, stage):
        l, n, e = self.l, self.n, self.e
        core, slot = l.core, lax.rem(c, SLOTS)
        if stage == 0:
            dst = self.landing.at[slot, :, pl.ds(0, PIECE)]
            return [self.make(self.g.at[c, :, 1 - core], dst, c, stage, 0, l.other_core)]
        if stage <= n:
            out = []
            for t in range(NT):
                own, partner = l.halving[l.orders[t][stage - 1]]
                rows = PIECE >> stage
                low = pl.multiple_of(self.span(t, stage - 1) + (1 - own) * rows, 16)
                src = self.g.at[c, t, core, pl.ds(low, rows)]
                dst = self.landing.at[slot, t, pl.ds(2 * PIECE - 2 * rows, rows)]
                out.append(self.make(src, dst, c, stage, t, partner))
            return out
        rows = PIECE >> n
        if stage <= n + e:
            partner = l.extra[stage - n - 1][1]
            out = []
            for t in range(NT):
                src = self.g.at[c, t, core, pl.ds(self.span(t, n), rows)]
                out.append(self.make(src, self.small.at[slot, stage - n - 1, t], c, stage, t, partner))
            return out
        k = 2 * n + e + 1 - stage
        if k > 0:
            out = []
            for t in range(NT):
                view = self.g.at[c, t, core, pl.ds(self.span(t, k), PIECE >> k)]
                out.append(self.make(view, view, c, stage, t, l.halving[l.orders[t][k - 1]][1]))
            return out
        view = self.g.at[c, :, core]
        return [self.make(view, view, c, stage, 0, l.other_core)]

    def make(self, src, dst, c, stage, t, partner):
        slot = lax.rem(c, SLOTS)
        return pltpu.make_async_remote_copy(
            src_ref=src, dst_ref=dst, send_sem=self.send.at[slot, stage, t], recv_sem=self.recv.at[slot, stage, t],
            device_id=partner, device_id_type=MESH)

    def fold(self, c, stage):
        n, e = self.n, self.e
        if stage > n + e:
            return
        core, slot = self.l.core, lax.rem(c, SLOTS)
        rows = PIECE >> min(stage, n)
        for t in range(NT):
            view = self.g.at[c, t, core, pl.ds(self.span(t, min(stage, n)), rows)]
            if stage <= n:
                got = self.landing[slot, t, pl.ds(0 if stage == 0 else 2 * PIECE - 2 * rows, rows)]
            else:
                got = self.small[slot, stage - n - 1, t]
            view[...] = (view[...].astype(F32) + got.astype(F32)).astype(BF)

    def partners(self, level):
        if level == 0:
            return [(0, self.l.other_core)]
        return [(t, self.l.halving[self.l.orders[t][level - 1]][1]) for t in range(NT)]

    def step(self, k, c):
        if k > 0:
            for copy in self.copies(c, k - 1):
                copy.wait()
            self.fold(c, k - 1)
            if k - 1 <= self.n:
                for t, partner in self.partners(k - 1):
                    pl.semaphore_signal(self.free.at[k - 1, t], inc=1, device_id=partner, device_id_type=MESH)
        if k < self.steps - 1:
            back = 2 * self.n + self.e + 1 - k
            if back <= self.n:
                for t, _ in self.partners(back):
                    pl.semaphore_wait(self.free.at[back, t], 1)
            for copy in self.copies(c, k):
                copy.start()

    def round(self, r, plan, finish):
        for k in reversed(range(self.steps)):
            c, valid = plan(r - k)

            @pl.when(valid)
            def _():
                self.step(k, c)
                if k == self.steps - 1:
                    finish(c)


def reducer_scratch(row_bits, chunks):
    n, e = min(3, row_bits + 1), max(0, row_bits - 2)
    stages = 2 + 2 * n + e
    return [
        pltpu.VMEM((chunks, NT, 2, PIECE, 128), BF),
        pltpu.VMEM((SLOTS, NT, 2 * PIECE - (PIECE >> n), 128), BF),
        pltpu.VMEM((SLOTS, max(e, 1), NT, PIECE >> n, 128), BF),
        pltpu.SemaphoreType.DMA((SLOTS, stages, NT)),
        pltpu.SemaphoreType.DMA((SLOTS, stages, NT)),
        pltpu.SemaphoreType.REGULAR((n + 1, NT)),
    ]


def half_of(pair, which):
    lane = lax.broadcasted_iota(jnp.int32, pair.shape, 1)
    return jnp.where((lane // HEAD_DIM) == which, pair, jnp.zeros_like(pair))


def inverse_rms(value):
    return lax.rsqrt(jnp.mean(value * value, axis=-1, keepdims=True) + EPSILON)


def layer_kernel(
    row_bits, sizes,
    blocks, ids, cotangent, w_qkv_hbm, w_out_hbm, gain_one, gain_two, w_gate, w_up, w_down,
    y_back, dx_back, summed, gain_sums,
    x_in, g_in, id_rows, id_q, id_k, n1_t, q, k, v, o_t, lse, x_one, n2, n2_t, acc, d_one, sent, part, w_qkv, w_out, gate_buf, up_buf, down_buf,
    dk_acc, dv_acc, gains, gains_in,
    grads, landing, small, send, recv, free,
    w_sem, ff_sem, own_sem, row_send, row_recv, out_sem, gain_send, gain_recv,
):
    tokens, positions, features, hidden, heads = sizes
    ff_chunks, groups, pairs = hidden // COLS, features // COLS, heads // 2
    count = tokens // positions
    out_chunk = ff_chunks
    chunks = ff_chunks + 1 + groups
    scale = HEAD_DIM ** (-0.5)
    scale_two = scale * 1.4426950408889634
    links = Links(row_bits)
    seq, row = links.seq, links.row
    reducer = Reducer(links, grads, landing, small, send, recv, free)

    def tile_of(d):
        return pl.ds(pl.multiple_of(links.peers[d] * positions, positions), positions)

    loads = [pltpu.make_async_copy(w_qkv_hbm.at[i], w_qkv.at[i], w_sem.at[i]) for i in range(3)]
    loads.append(pltpu.make_async_copy(w_out_hbm, w_out, w_sem.at[3]))
    mine = tile_of(0)
    own_ids = pl.ds(pl.multiple_of(seq * 8, 8), 8)
    own = [
        pltpu.make_async_copy(blocks.at[seq], x_in.at[mine], own_sem.at[0]),
        pltpu.make_async_copy(ids.at[seq], id_rows.at[own_ids], own_sem.at[1]),
        pltpu.make_async_copy(cotangent.at[seq], g_in.at[mine], own_sem.at[2]),
    ]
    own[0].start()
    for copy in loads:
        copy.start()
    own[1].start()
    own[2].start()
    links.greet()

    def to_peer(a, d, src, dst):
        return pltpu.make_async_remote_copy(
            src_ref=src, dst_ref=dst, send_sem=row_send.at[a, d], recv_sem=row_recv.at[a, d],
            device_id=(links.peers[d], row), device_id_type=MESH)

    x_moves = [to_peer(0, d, blocks.at[links.peers[d]], x_in.at[mine]) for d in range(1, count)]
    id_moves = [to_peer(1, d, ids.at[links.peers[d]], id_rows.at[own_ids]) for d in range(1, count)]
    g_moves = [to_peer(2, d, cotangent.at[links.peers[d]], g_in.at[mine]) for d in range(1, count)]
    for copy in x_moves + id_moves:
        copy.start()

    own[0].wait()
    for copy in loads[:3]:
        copy.wait()
    for d in range(count):
        if d > 0:
            x_moves[d - 1].wait()
        if d == count - 1:
            for copy in g_moves:
                copy.start()
        tile = tile_of(d)
        value = x_in[tile, :].astype(F32)
        normed = (value * inverse_rms(value) * gain_one[...]).astype(BF)
        n1_t[:, tile] = normed.T
        for i, made in enumerate((q, k, v)):
            made[tile, :] = dot(normed, w_qkv[i]).astype(BF)

    own[1].wait()
    for copy in id_moves:
        copy.wait()
    for d in range(count):
        id_q[:, positions * d : positions * (d + 1)] = id_rows[8 * d : 8 * d + 8, :]
    for j in range(tokens // 128):
        block = jnp.broadcast_to(id_q[0:1, 128 * j : 128 * j + 128], (128, 128))
        id_k[128 * j : 128 * j + 128, :] = block.T

    def masked(scores, queries, width):
        same = jnp.concatenate([id_k[...]] * (width // 128), axis=1) == id_q[0:1, queries]
        return jnp.where(same, scores, MASKED)

    def forward_pair(p, _):
        cols = pl.ds(pl.multiple_of(p * 128, 128), 128)
        key_pair = k[:, cols]
        value_t = v[:, cols].T
        for h in range(2):
            key = half_of(key_pair, h)
            rows = pl.ds(pl.multiple_of(p * 128 + HEAD_DIM * h, HEAD_DIM), HEAD_DIM)
            scores = masked(dot(key, q[:, cols], NTRANS) * scale_two, slice(None), tokens)
            largest = jnp.max(scores, axis=0, keepdims=True)
            exponent = jnp.exp2(scores - largest)
            total = jnp.sum(exponent, axis=0, keepdims=True)
            mixed = dot(value_t[HEAD_DIM * h : HEAD_DIM * (h + 1)], exponent.astype(BF))
            o_t[rows, :] = (mixed / total).astype(BF)
            lse[p * 2 + h, 0:1, :] = largest + jnp.log2(total)
        return 0

    lax.fori_loop(0, pairs, forward_pair, 0)

    def ff_loads(c):
        slot = lax.rem(c, 2)
        cols = pl.ds(pl.multiple_of(c * COLS, COLS), COLS)
        return [
            pltpu.make_async_copy(w_gate.at[:, cols], gate_buf.at[slot], ff_sem.at[slot, 0]),
            pltpu.make_async_copy(w_up.at[:, cols], up_buf.at[slot], ff_sem.at[slot, 1]),
            pltpu.make_async_copy(w_down.at[cols, :], down_buf.at[slot], ff_sem.at[slot, 2]),
        ]

    for copy in ff_loads(0):
        copy.start()

    loads[3].wait()

    def project_tile(i, _):
        tile = pl.ds(pl.multiple_of(i * positions, positions), positions)
        mixed = o_t[:, tile].T
        value = x_in[tile, :].astype(F32) + dot(mixed, w_out[...])
        normed = (value * inverse_rms(value) * gain_two[...]).astype(BF)
        x_one[tile, :] = value
        acc[tile, :] = value
        n2[tile, :] = normed
        n2_t[:, tile] = normed.T
        d_one[tile, :] = jnp.zeros((positions, features), F32)
        return 0

    lax.fori_loop(0, count, project_tile, 0)
    own[2].wait()
    for copy in g_moves:
        copy.wait()

    first = out_chunk + 2

    def plan(u):
        late = u - first
        chunk = jnp.where(u <= out_chunk, u, out_chunk + 1 + late // 2)
        valid = (u >= 0) & ((u <= out_chunk) | ((late >= 0) & (late <= 2 * (groups - 1)) & (lax.rem(late, 2) == 0)))
        return chunk, valid

    def finish(c):
        pltpu.make_async_copy(grads.at[c], summed.at[c], out_sem.at[c]).start()

    def put(c, t, piece):
        for half in range(2):
            grads[c, t, half] = piece[:, 128 * half : 128 * half + 128].astype(BF)

    half_tokens = tokens // 2

    def ff_chunk(c, _):
        slot = lax.rem(c, 2)

        @pl.when(c + 1 < ff_chunks)
        def _():
            for copy in ff_loads(c + 1):
                copy.start()

        for copy in ff_loads(c):
            copy.wait()
        for i in range(2):
            tile = slice(half_tokens * i, half_tokens * (i + 1))
            gate = dot(n2[tile, :], gate_buf[slot])
            up = dot(n2[tile, :], up_buf[slot])
            d_hidden = dot(g_in[tile, :], down_buf[slot], NTRANS)
            square = gate * gate
            bend = 0.7978845608028654 * 0.044715
            turn = jnp.tanh(gate * (0.7978845608028654 + bend * square))
            rise = 0.5 + 0.5 * turn
            activated = gate * rise
            slope = rise + 0.5 * gate * (1.0 - turn * turn) * (0.7978845608028654 + 3.0 * bend * square)
            low_h = (activated * up).astype(BF)
            low_gate = (d_hidden * up * slope).astype(BF)
            low_up = (d_hidden * activated).astype(BF)
            part[0, tile, :] = low_gate
            part[1, tile, :] = low_up
            part[2, tile, :] = low_h
            acc[tile, :] += dot(low_h, down_buf[slot])
            d_one[tile, :] += dot(low_gate, gate_buf[slot], NTRANS) + dot(low_up, up_buf[slot], NTRANS)
        put(c, 0, dot(n2_t[...], part[0]))
        put(c, 1, dot(n2_t[...], part[1]))
        made = dot(part[2].T, g_in[...])
        for j in range(NT):
            for half in range(2):
                at = COLS * j + 128 * half
                grads[c, 2, half, COLS * j : COLS * (j + 1), :] = made[:, at : at + 128].astype(BF)
        reducer.round(c, plan, finish)
        return 0

    lax.fori_loop(0, ff_chunks, ff_chunk, 0)

    gains[...] = jnp.zeros_like(gains)
    local = []
    y_moves = []
    for d in range(count):
        tile = tile_of(d)
        sent[tile, :] = acc[tile, :].astype(BF)
        if d == 0:
            copy = pltpu.make_async_copy(sent.at[tile], y_back.at[seq], own_sem.at[0])
            local.append(copy)
        else:
            copy = to_peer(0, d, sent.at[tile], y_back.at[seq])
            y_moves.append(copy)
        copy.start()
    for d in range(count):
        tile = tile_of(d)
        value = x_one[tile, :]
        inverse = inverse_rms(value)
        slope = d_one[tile, :]
        hat = value * inverse
        gains[1:2, :] += jnp.sum(slope * hat, axis=0, keepdims=True)
        weighted = slope * gain_two[...]
        pulled = inverse * (weighted - hat * jnp.mean(weighted * hat, axis=-1, keepdims=True))
        total = g_in[tile, :].astype(F32) + pulled
        d_one[tile, :] = total
        low = total.astype(BF)
        g_in[tile, :] = low
        d_mixed = dot(low, w_out[...], NTRANS).astype(BF)
        n2[tile, :] = d_mixed
        n2_t[:, tile] = d_mixed.T
    for t in range(NT):
        put(out_chunk, t, dot(o_t[...], g_in[:, COLS * t : COLS * (t + 1)]))
    reducer.round(jnp.int32(out_chunk), plan, finish)

    width = 256

    def backward_pair(step, _):
        g, j = step // 2, lax.rem(step, 2)
        cols = pl.ds(pl.multiple_of(step * 128, 128), 128)
        key_pair, value_pair = k[:, cols], v[:, cols]
        key_t = key_pair.T
        dq = []
        for h in range(2):
            key, value = half_of(key_pair, h), half_of(value_pair, h)
            rows = pl.ds(pl.multiple_of(step * 128 + HEAD_DIM * h, HEAD_DIM), HEAD_DIM)
            dq_parts = []
            for i in range(tokens // width):
                qs = slice(width * i, width * (i + 1))
                scores = masked(dot(key, q[qs, cols], NTRANS) * scale_two, qs, width)
                prob = jnp.exp2(scores - lse[step * 2 + h, 0:1, qs])
                delta = jnp.sum(n2_t[rows, qs].astype(F32) * o_t[rows, qs].astype(F32), axis=0, keepdims=True)
                d_prob = dot(value, n2[qs, cols], NTRANS)
                d_score = (prob * (d_prob - delta)).astype(BF)
                low = prob.astype(BF)
                dv = dot(low, n2[qs, cols])
                dk = dot(d_score, q[qs, cols])
                if i == 0:
                    dv_acc[h] = dv
                    dk_acc[h] = dk
                else:
                    dv_acc[h] += dv
                    dk_acc[h] += dk
                dq_parts.append((dot(key_t[HEAD_DIM * h : HEAD_DIM * (h + 1)], d_score) * scale).astype(BF))
            dq.append(jnp.concatenate(dq_parts, axis=1))
        lane = lax.broadcasted_iota(jnp.int32, (tokens, 128), 1) < HEAD_DIM
        at = pl.ds(pl.multiple_of(j * 128, 128), 128)
        part[0, :, at] = jnp.concatenate(dq, axis=0).T
        part[1, :, at] = (jnp.where(lane, dk_acc[0], dk_acc[1]) * scale).astype(BF)
        part[2, :, at] = jnp.where(lane, dv_acc[0], dv_acc[1]).astype(BF)

        @pl.when(j == 1)
        def _():
            group = pl.ds(pl.multiple_of(g * COLS, COLS), COLS)
            for t in range(NT):
                put(out_chunk + 1 + g, t, dot(n1_t[...], part[t]))
            for d in range(count):
                tile = slice(positions * d, positions * (d + 1))
                back = sum(dot(part[t, tile, :], w_qkv[t, :, group], NTRANS) for t in range(NT))

                @pl.when(g == 0)
                def _():
                    acc[tile, :] = back

                @pl.when(g > 0)
                def _():
                    acc[tile, :] += back

        reducer.round(out_chunk + 1 + step, plan, finish)
        return 0

    lax.fori_loop(0, pairs, backward_pair, 0)

    for copy in local + y_moves:
        copy.wait()
    dx_moves = []
    for d in range(count):
        tile = tile_of(d)
        value = x_in[tile, :].astype(F32)
        inverse = inverse_rms(value)
        slope = acc[tile, :]
        hat = value * inverse
        gains[0:1, :] += jnp.sum(slope * hat, axis=0, keepdims=True)
        weighted = slope * gain_one[...]
        pulled = inverse * (weighted - hat * jnp.mean(weighted * hat, axis=-1, keepdims=True))
        sent[tile, :] = (d_one[tile, :] + pulled).astype(BF)
        if d == 0:
            copy = pltpu.make_async_copy(sent.at[tile], dx_back.at[seq], own_sem.at[1])
        else:
            copy = to_peer(1, d, sent.at[tile], dx_back.at[seq])
        copy.start()
        dx_moves.append(copy)

    axes = links.all()

    def gain_copy(i):
        return pltpu.make_async_remote_copy(
            src_ref=gains, dst_ref=gains_in.at[i], send_sem=gain_send.at[i], recv_sem=gain_recv.at[i],
            device_id=axes[i], device_id_type=MESH)

    begin = out_chunk + 1 + pairs
    last = first + 2 * (groups - 1) + reducer.steps - 1

    def tail(r, _):
        for i in range(len(axes) + 1):

            @pl.when(r == begin + i)
            def _():
                if i > 0:
                    gain_copy(i - 1).wait()
                    gains[...] += gains_in[i - 1]
                if i < len(axes):
                    gain_copy(i).start()

        reducer.round(r, plan, finish)
        return 0

    lax.fori_loop(begin, max(last + 1, begin + len(axes) + 1), tail, 0)
    gain_sums[...] = gains[...]
    for copy in dx_moves:
        copy.wait()
    for c in range(chunks):
        pltpu.make_async_copy(grads.at[c], summed.at[c], out_sem.at[c]).wait()


def run_layer(row_bits, blocks, ids, cotangent, w_qkv, w_out, gain_one, gain_two, w_gate, w_up, w_down):
    count, positions, features = blocks.shape
    hidden = w_gate.shape[1]
    tokens, heads = count * positions, features // HEAD_DIM
    chunks = hidden // COLS + 1 + features // COLS
    axes = row_bits + 2
    sizes = (tokens, positions, features, hidden, heads)
    anywhere, inside = pl.BlockSpec(memory_space=pl.ANY), pl.BlockSpec(memory_space=pltpu.VMEM)
    back = jax.ShapeDtypeStruct(blocks.shape, BF)
    low = pltpu.VMEM((tokens, features), BF)
    turned = pltpu.VMEM((features, tokens), BF)
    full = pltpu.VMEM((tokens, features), F32)
    dma = pltpu.SemaphoreType.DMA
    return pl.pallas_call(
        partial(layer_kernel, row_bits, sizes),
        out_shape=(back, back, jax.ShapeDtypeStruct((chunks, NT, 2, PIECE, 128), BF), jax.ShapeDtypeStruct((8, features), F32)),
        in_specs=[anywhere] * 5 + [inside] * 2 + [anywhere] * 3,
        out_specs=[anywhere] * 3 + [inside],
        scratch_shapes=[
            low, low,
            pltpu.VMEM((count * 8, positions), jnp.int32), pltpu.VMEM((8, tokens), jnp.int32), pltpu.VMEM((tokens, 128), jnp.int32),
            turned, low, low, low, turned, pltpu.VMEM((heads, 8, tokens), F32), full, low, turned, full, full, low,
            pltpu.VMEM((NT, tokens, COLS), BF),
            pltpu.VMEM((3, features, features), BF), pltpu.VMEM((features, features), BF),
            pltpu.VMEM((2, features, COLS), BF), pltpu.VMEM((2, features, COLS), BF), pltpu.VMEM((2, COLS, features), BF),
            pltpu.VMEM((2, tokens, 128), F32), pltpu.VMEM((2, tokens, 128), F32),
            pltpu.VMEM((8, features), F32), pltpu.VMEM((axes, 8, features), F32),
        ] + reducer_scratch(row_bits, chunks) + [
            dma((4,)), dma((2, 3)), dma((3,)), dma((3, count)), dma((3, count)), dma((chunks,)), dma((axes,)), dma((axes,)),
        ],
        compiler_params=pltpu.CompilerParams(collective_id=0, has_side_effects=True, vmem_limit_bytes=63 * 2**20),
        cost_estimate=pl.CostEstimate(flops=60 * 10**9, bytes_accessed=60 * 10**6, transcendentals=10**7),
    )(blocks, ids, cotangent, w_qkv, w_out, gain_one, gain_two, w_gate, w_up, w_down)


def widen_ff_kernel(low, gate, up, down):
    for half in range(2):
        cols = slice(128 * half, 128 * half + 128)
        gate[:, cols] = low[0, 0, half].astype(F32)
        up[:, cols] = low[0, 1, half].astype(F32)
        for j in range(NT):
            down[:, COLS * j + 128 * half : COLS * j + 128 * half + 128] = low[0, 2, half, COLS * j : COLS * (j + 1), :].astype(F32)


def widen_ff(summed, features, hidden):
    return pl.pallas_call(
        widen_ff_kernel,
        grid=(hidden // COLS,),
        out_shape=(jax.ShapeDtypeStruct((features, hidden), F32),) * 2 + (jax.ShapeDtypeStruct((hidden, features), F32),),
        in_specs=[pl.BlockSpec((1, NT, 2, PIECE, 128), lambda c: (c, 0, 0, 0, 0))],
        out_specs=[pl.BlockSpec((features, COLS), lambda c: (0, c))] * 2 + [pl.BlockSpec((COLS, features), lambda c: (c, 0))],
    )(summed)


def widen_square_kernel(low_out, low_qkv, g_out, g_q, g_k, g_v):
    for half in range(2):
        cols = slice(128 * half, 128 * half + 128)
        g_out[:, cols] = low_out[0, 0, half].astype(F32)
        for t, made in enumerate((g_q, g_k, g_v)):
            made[:, cols] = low_qkv[0, t, half].astype(F32)


def widen_square(summed, features, first):
    wide = pl.BlockSpec((features, COLS), lambda j: (0, j))
    return pl.pallas_call(
        widen_square_kernel,
        grid=(features // COLS,),
        out_shape=(jax.ShapeDtypeStruct((features, features), F32),) * 4,
        in_specs=[
            pl.BlockSpec((1, 1, 2, PIECE, 128), lambda j: (first, j, 0, 0, 0)),
            pl.BlockSpec((1, NT, 2, PIECE, 128), lambda j: (first + 1 + j, 0, 0, 0, 0)),
        ],
        out_specs=[wide] * 4,
    )(summed, summed)


def body(row_bits, blocks, segment_ids, cotangent, w_query, w_key, w_value, w_out, norm_one, norm_two, w_gate, w_up, w_down):
    count, positions, features = blocks.shape
    hidden = w_gate.shape[1]
    ids = jnp.broadcast_to(segment_ids[:, None, :], (count, 8, positions))
    y, dx, summed, gains = run_layer(
        row_bits, blocks, ids, cotangent, jnp.stack([w_query, w_key, w_value]), w_out,
        norm_one.reshape(1, features), norm_two.reshape(1, features), w_gate, w_up, w_down)
    g_gate, g_up, g_down = widen_ff(summed, features, hidden)
    g_out, g_q, g_k, g_v = widen_square(summed, features, hidden // COLS)
    return (y, dx, g_q, g_k, g_v, g_out, gains[0], gains[1], g_gate, g_up, g_down)


def solution(mesh):
    split = P("rows", "seq", None)
    row_bits = (mesh.shape["rows"] - 1).bit_length()
    return jax.shard_map(
        partial(body, row_bits),
        mesh=mesh,
        in_specs=(split, P("rows", "seq"), split) + (P(),) * 9,
        out_specs=(split, split) + (P(),) * 9,
        check_vma=False,
    )
```

time: 794 us -> 255 us (0.32)
  local copies, waits for them, and re-layouts: 253 us -> 8.38 us
  matrix products: 188 us -> 0 us
  other arithmetic: 104 us -> 3.4 us
  Pallas kernels: 201 us -> 242 us
  blocking collectives: 40 us -> 0 us
    dot_general x26 -> x0, matrix products: 162 us -> none  [the longest x1 25.4 us: body(): jnp.einsum('qhd,khd->hqk', d_mixed, value, preferred_element_type=jnp.flo...]
    transpose x46 -> x0, local copies, waits for them, and re-layouts: 104 us -> none  [the longest x38 91.5 us: whole(): return pair.transpose(1, 0, 2).reshape(PIECE, 256)]
    unnamed x231 -> x6, local copies, waits for them, and re-layouts: 103 us -> 3.12 us
    convert_element_type x5 -> x0, other arithmetic: 88.5 us -> none  [the longest x1 40.9 us: body(): (wide * (d_probs - jnp.sum(wide * d_probs, axis=-1, keepdims=True))).asty...]
    pallas_call x2 -> x3, Pallas kernels: 201 us -> 242 us  [the longest x1 225 us: run_layer(): pl.pallas_call(partial(layer_kernel, row_bits, sizes), out_shape=(back, b...]
    psum x1 -> x0, blocking collectives: 40 us -> none  [body(): gains = lax.psum(jnp.stack([d_norm_one, d_norm_two]), ('seq', 'rows'))]
    sub x1 -> x0, matrix products: 25.7 us -> none  [body(): exponent = jnp.exp(scores - jnp.max(scores, axis=-1, keepdims=True))]
    convert_element_type x12 -> x0, local copies, waits for them, and re-layouts: 21.5 us -> none  [halves(): return piece.reshape(PIECE, 2, 128).transpose(1, 0, 2).astype(jnp.bfloat16)]
where the time goes in v2:
time: 255 us
  Pallas kernels  242 us (95%)
  local copies, waits for them, and re-layouts  8.38 us (3%)
  other arithmetic  3.4 us (1%)
    pallas_call x1, Pallas kernels, run_layer(): pl.pallas_call(partial(layer_kernel, row_bits, sizes), out_shape=(back, b...  225 us
    pallas_call x1, Pallas kernels, widen_ff(): pl.pallas_call(widen_ff_kernel, grid=(hidden // COLS,), out_shape=(jax.Sh...  11.3 us
    pallas_call x1, Pallas kernels, widen_square(): pl.pallas_call(widen_square_kernel, grid=(features // COLS,), out_shape=(...  6.06 us

profile of v2, /device:TPU:0, one launch (start us, length us, event | category | flops | bytes accessed | tf_op | source)
XLA Modules:
  0.0 254.7 jit_solution(3725353892040308159)
XLA Ops:
  0.6 1.3 reshape.29.gain_one
  1.9 1.3 reshape.30.gain_two
  3.2 1.3 broadcast_in_dim.2.ids
  4.5 3.4 %pad_maximum_fusion.w_qkv_hbm = bf16[3,768,768]{2,1,0:T(8,128)(2,1)} fusion(bf16[1,768,768]{2,1,0:T(8,128)(2,1)} %bitcast.3, bf16[1,768,768]{2,1,0:T(8,128)(2,1)} %bitcast.4, bf16[1,768,768]{2,1,0:T(8,128)(2,1)} %bitcast.5), kind=kLoop, calls=%fused_computation | loop fusion | flops 3538944 | bytes 7077888 | tf_op jit(solution)/shard_map/stack | solution.py:596
  7.9 224.9 %shard_map.203 = (bf16[4,256,768]{2,1,0:T(8,128)(2,1)}, bf16[4,256,768]{2,1,0:T(8,128)(2,1)}, bf16[12,3,2,768,128]{4,3,2,1,0:T(8,128)(2,1)}, f32[8,768]{1,0:T(8,128)}) custom-call(bf16[4,256,768]{2,1,0:T(8,128)(2,1)} %blocks.1, s32[4,8,256]{2,1,0:T(8,128)} %broadcast_in_dim.2.ids, bf16[4,256,768]{2,1,0:T(8,128)(2,1)} %cotangent.1, ...), custom_call_target="tpu_custom_call" | custom-call | flops 60000002048 | bytes 60000000 | tf_op jit(solution)/shard_map/pallas_call | solution.py:528
  232.8 1.4 slice_reduce_fusion
  234.2 6.1 %shard_map.204 = (f32[768,768]{1,0:T(8,128)}, f32[768,768]{1,0:T(8,128)}, f32[768,768]{1,0:T(8,128)}, f32[768,768]{1,0:T(8,128)}) custom-call(bf16[12,3,2,768,128]{4,3,2,1,0:T(8,128)(2,1)} %get-tuple-element.24.low_out.low_qkv.low, bf16[12,3,2,768,128]{4,3,2,1,0:T(8,128)(2,1)} %get-tuple-element.24.low_out.low_qkv.low), custom_call_target="tpu_custom_call" | custom-call | tf_op jit(solution)/shard_map/pallas_call | solution.py:579
  240.3 0.0 copy-start.1
  240.3 11.3 %shard_map.205 = (f32[768,2048]{1,0:T(8,128)}, f32[768,2048]{1,0:T(8,128)}, f32[2048,768]{1,0:T(8,128)}) custom-call(bf16[12,3,2,768,128]{4,3,2,1,0:T(8,128)(2,1)} %get-tuple-element.24.low_out.low_qkv.low), custom_call_target="tpu_custom_call" | custom-call | tf_op jit(solution)/shard_map/pallas_call | solution.py:560
  251.6 0.0 copy-start
  251.6 0.0 copy-done.1
  251.6 1.1 copy.25
  252.7 0.8 copy-done
  253.6 1.1 copy.26
Async XLA Ops:
  240.3 11.3 %copy-start.1 = (bf16[4,256,768]{2,1,0:T(8,128)(2,1)S(1)}, bf16[4,256,768]{2,1,0:T(8,128)(2,1)}, u32[]{:S(2)}) copy-start(bf16[4,256,768]{2,1,0:T(8,128)(2,1)} %get-tuple-element.46) | copy-start | bytes 4718596
  251.6 2.0 copy-start

commit v3 on v2

--- a/solution.py
+++ b/solution.py
@@ -14,7 +14,10 @@
 PIECE = 768
 NT = 3
 COLS = 256
-SLOTS = 3
+SLOTS = 4
+GAP = 2
+Y_PIECES = 8
+X_PIECES = 16
 BF = jnp.bfloat16
 F32 = jnp.float32
 NN = (((1,), (0,)), ((), ()))
@@ -67,7 +70,6 @@
         self.send, self.recv, self.free = send, recv, free
         n, e = len(links.halving), len(links.extra)
         self.n, self.e = n, e
-        self.steps = 2 + 2 * n + e + 1
 
     def span(self, t, level):
         low = 0
@@ -127,14 +129,14 @@
                 got = self.landing[slot, t, pl.ds(0 if stage == 0 else 2 * PIECE - 2 * rows, rows)]
             else:
                 got = self.small[slot, stage - n - 1, t]
-            view[...] = (view[...].astype(F32) + got.astype(F32)).astype(BF)
+            view[...] = view[...] + got
 
     def partners(self, level):
         if level == 0:
             return [(0, self.l.other_core)]
         return [(t, self.l.halving[self.l.orders[t][level - 1]][1]) for t in range(NT)]
 
-    def step(self, k, c):
+    def shrink(self, k, c):
         if k > 0:
             for copy in self.copies(c, k - 1):
                 copy.wait()
@@ -142,22 +144,34 @@
             if k - 1 <= self.n:
                 for t, partner in self.partners(k - 1):
                     pl.semaphore_signal(self.free.at[k - 1, t], inc=1, device_id=partner, device_id_type=MESH)
-        if k < self.steps - 1:
-            back = 2 * self.n + self.e + 1 - k
-            if back <= self.n:
-                for t, _ in self.partners(back):
-                    pl.semaphore_wait(self.free.at[back, t], 1)
+        if k <= self.n + self.e:
             for copy in self.copies(c, k):
                 copy.start()
 
-    def round(self, r, plan, finish):
-        for k in reversed(range(self.steps)):
-            c, valid = plan(r - k)
+    def spread(self, j, c):
+        stage = self.n + self.e + 1 + j
+        if j > 0:
+            for copy in self.copies(c, stage - 1):
+                copy.wait()
+        if j <= self.n:
+            for t, _ in self.partners(self.n - j):
+                pl.semaphore_wait(self.free.at[self.n - j, t], 1)
+            for copy in self.copies(c, stage):
+                copy.start()
+
+    def shrink_round(self, u, plan):
+        for k in reversed(range(self.n + self.e + 2)):
+            c, valid = plan(u - GAP * k)
+            pl.when(valid)(partial(self.shrink, k, c))
+
+    def spread_round(self, u, plan, finish):
+        for j in reversed(range(self.n + 2)):
+            c, valid = plan(u - GAP * j)
 
             @pl.when(valid)
             def _():
-                self.step(k, c)
-                if k == self.steps - 1:
+                self.spread(j, c)
+                if j == self.n + 1:
                     finish(c)
 
 
@@ -185,7 +199,7 @@
 
 def layer_kernel(
     row_bits, sizes,
-    blocks, ids, cotangent, w_qkv_hbm, w_out_hbm, gain_one, gain_two, w_gate, w_up, w_down,
+    blocks, ids, cotangent, w_q_hbm, w_k_hbm, w_v_hbm, w_out_hbm, gain_one, gain_two, w_gate, w_up, w_down,
     y_back, dx_back, summed, gain_sums,
     x_in, g_in, id_rows, id_q, id_k, n1_t, q, k, v, o_t, lse, x_one, n2, n2_t, acc, d_one, sent, part, w_qkv, w_out, gate_buf, up_buf, down_buf,
     dk_acc, dv_acc, gains, gains_in,
@@ -206,13 +220,12 @@
     def tile_of(d):
         return pl.ds(pl.multiple_of(links.peers[d] * positions, positions), positions)
 
-    loads = [pltpu.make_async_copy(w_qkv_hbm.at[i], w_qkv.at[i], w_sem.at[i]) for i in range(3)]
+    loads = [pltpu.make_async_copy(w, w_qkv.at[i], w_sem.at[i]) for i, w in enumerate((w_q_hbm, w_k_hbm, w_v_hbm))]
     loads.append(pltpu.make_async_copy(w_out_hbm, w_out, w_sem.at[3]))
     mine = tile_of(0)
-    own_ids = pl.ds(pl.multiple_of(seq * 8, 8), 8)
     own = [
         pltpu.make_async_copy(blocks.at[seq], x_in.at[mine], own_sem.at[0]),
-        pltpu.make_async_copy(ids.at[seq], id_rows.at[own_ids], own_sem.at[1]),
+        pltpu.make_async_copy(ids, id_rows.at[seq], own_sem.at[1]),
         pltpu.make_async_copy(cotangent.at[seq], g_in.at[mine], own_sem.at[2]),
     ]
     own[0].start()
@@ -228,7 +241,7 @@
             device_id=(links.peers[d], row), device_id_type=MESH)
 
     x_moves = [to_peer(0, d, blocks.at[links.peers[d]], x_in.at[mine]) for d in range(1, count)]
-    id_moves = [to_peer(1, d, ids.at[links.peers[d]], id_rows.at[own_ids]) for d in range(1, count)]
+    id_moves = [to_peer(1, d, ids, id_rows.at[seq]) for d in range(1, count)]
     g_moves = [to_peer(2, d, cotangent.at[links.peers[d]], g_in.at[mine]) for d in range(1, count)]
     for copy in x_moves + id_moves:
         copy.start()
@@ -244,7 +257,7 @@
                 copy.start()
         tile = tile_of(d)
         value = x_in[tile, :].astype(F32)
-        normed = (value * inverse_rms(value) * gain_one[...]).astype(BF)
+        normed = (value * inverse_rms(value) * gain_one[...].reshape(1, features)).astype(BF)
         n1_t[:, tile] = normed.T
         for i, made in enumerate((q, k, v)):
             made[tile, :] = dot(normed, w_qkv[i]).astype(BF)
@@ -253,7 +266,7 @@
     for copy in id_moves:
         copy.wait()
     for d in range(count):
-        id_q[:, positions * d : positions * (d + 1)] = id_rows[8 * d : 8 * d + 8, :]
+        id_q[0:1, positions * d : positions * (d + 1)] = id_rows[d, pl.ds(seq, 1), :]
     for j in range(tokens // 128):
         block = jnp.broadcast_to(id_q[0:1, 128 * j : 128 * j + 128], (128, 128))
         id_k[128 * j : 128 * j + 128, :] = block.T
@@ -298,7 +311,7 @@
         tile = pl.ds(pl.multiple_of(i * positions, positions), positions)
         mixed = o_t[:, tile].T
         value = x_in[tile, :].astype(F32) + dot(mixed, w_out[...])
-        normed = (value * inverse_rms(value) * gain_two[...]).astype(BF)
+        normed = (value * inverse_rms(value) * gain_two[...].reshape(1, features)).astype(BF)
         x_one[tile, :] = value
         acc[tile, :] = value
         n2[tile, :] = normed
@@ -311,13 +324,21 @@
     for copy in g_moves:
         copy.wait()
 
-    first = out_chunk + 2
-
-    def plan(u):
-        late = u - first
-        chunk = jnp.where(u <= out_chunk, u, out_chunk + 1 + late // 2)
-        valid = (u >= 0) & ((u <= out_chunk) | ((late >= 0) & (late <= 2 * (groups - 1)) & (lax.rem(late, 2) == 0)))
+    down = reducer.n + reducer.e + 1
+    late_down = out_chunk + 4
+
+    def shrink_plan(u):
+        late = u - late_down
+        chunk = jnp.where(u <= out_chunk, u, out_chunk + 1 + late // 4)
+        valid = (u >= 0) & ((u <= out_chunk) | ((late >= 0) & (late <= 4 * (groups - 1)) & (lax.rem(late, 4) == 0)))
         return chunk, valid
+
+    def spread_plan(u):
+        return shrink_plan(u - GAP * down)
+
+    def advance(u):
+        reducer.shrink_round(u, shrink_plan)
+        reducer.spread_round(u, spread_plan, finish)
 
     def finish(c):
         pltpu.make_async_copy(grads.at[c], summed.at[c], out_sem.at[c]).start()
@@ -364,23 +385,29 @@
             for half in range(2):
                 at = COLS * j + 128 * half
                 grads[c, 2, half, COLS * j : COLS * (j + 1), :] = made[:, at : at + 128].astype(BF)
-        reducer.round(c, plan, finish)
+        reducer.shrink_round(c, shrink_plan)
         return 0
 
     lax.fori_loop(0, ff_chunks, ff_chunk, 0)
 
     gains[...] = jnp.zeros_like(gains)
-    local = []
-    y_moves = []
     for d in range(count):
         tile = tile_of(d)
         sent[tile, :] = acc[tile, :].astype(BF)
-        if d == 0:
-            copy = pltpu.make_async_copy(sent.at[tile], y_back.at[seq], own_sem.at[0])
-            local.append(copy)
-        else:
-            copy = to_peer(0, d, sent.at[tile], y_back.at[seq])
-            y_moves.append(copy)
+
+    def whole_back(a, dst):
+        own_copy = pltpu.make_async_copy(sent.at[mine], dst.at[seq], own_sem.at[a])
+        return [own_copy] + [to_peer(a, d, sent.at[tile_of(d)], dst.at[seq]) for d in range(1, count)]
+
+    def piece_back(a, dst, i, pieces):
+        rows = positions // pieces
+        for d in range(2, count):
+            low = pl.multiple_of(links.peers[d] * positions + i * rows, 16)
+            to = pl.ds(pl.multiple_of(i * rows, 16), rows)
+            to_peer(a, d, sent.at[pl.ds(low, rows)], dst.at[seq, to]).start()
+
+    y_moves = whole_back(0, y_back)
+    for copy in y_moves[:2]:
         copy.start()
     for d in range(count):
         tile = tile_of(d)
@@ -389,7 +416,7 @@
         slope = d_one[tile, :]
         hat = value * inverse
         gains[1:2, :] += jnp.sum(slope * hat, axis=0, keepdims=True)
-        weighted = slope * gain_two[...]
+        weighted = slope * gain_two[...].reshape(1, features)
         pulled = inverse * (weighted - hat * jnp.mean(weighted * hat, axis=-1, keepdims=True))
         total = g_in[tile, :].astype(F32) + pulled
         d_one[tile, :] = total
@@ -400,7 +427,7 @@
         n2_t[:, tile] = d_mixed.T
     for t in range(NT):
         put(out_chunk, t, dot(o_t[...], g_in[:, COLS * t : COLS * (t + 1)]))
-    reducer.round(jnp.int32(out_chunk), plan, finish)
+    reducer.shrink_round(jnp.int32(out_chunk), shrink_plan)
 
     width = 256
 
@@ -432,53 +459,48 @@
                     dk_acc[h] += dk
                 dq_parts.append((dot(key_t[HEAD_DIM * h : HEAD_DIM * (h + 1)], d_score) * scale).astype(BF))
             dq.append(jnp.concatenate(dq_parts, axis=1))
+            if h == 0:
+                advance(out_chunk + 1 + 2 * step)
+
+                @pl.when(step < Y_PIECES // 2)
+                def _():
+                    piece_back(0, y_back, 2 * step, Y_PIECES)
         lane = lax.broadcasted_iota(jnp.int32, (tokens, 128), 1) < HEAD_DIM
-        at = pl.ds(pl.multiple_of(j * 128, 128), 128)
-        part[0, :, at] = jnp.concatenate(dq, axis=0).T
-        part[1, :, at] = (jnp.where(lane, dk_acc[0], dk_acc[1]) * scale).astype(BF)
-        part[2, :, at] = jnp.where(lane, dv_acc[0], dv_acc[1]).astype(BF)
+        q[:, cols] = jnp.concatenate(dq, axis=0).T
+        k[:, cols] = (jnp.where(lane, dk_acc[0], dk_acc[1]) * scale).astype(BF)
+        v[:, cols] = jnp.where(lane, dv_acc[0], dv_acc[1]).astype(BF)
 
         @pl.when(j == 1)
         def _():
             group = pl.ds(pl.multiple_of(g * COLS, COLS), COLS)
-            for t in range(NT):
-                put(out_chunk + 1 + g, t, dot(n1_t[...], part[t]))
-            for d in range(count):
-                tile = slice(positions * d, positions * (d + 1))
-                back = sum(dot(part[t, tile, :], w_qkv[t, :, group], NTRANS) for t in range(NT))
-
-                @pl.when(g == 0)
-                def _():
-                    acc[tile, :] = back
-
-                @pl.when(g > 0)
-                def _():
-                    acc[tile, :] += back
-
-        reducer.round(out_chunk + 1 + step, plan, finish)
+            for t, made in enumerate((q, k, v)):
+                put(out_chunk + 1 + g, t, dot(n1_t[...], made[:, group]))
+
+        advance(out_chunk + 2 + 2 * step)
+
+        @pl.when(step < Y_PIECES // 2)
+        def _():
+            piece_back(0, y_back, 2 * step + 1, Y_PIECES)
+
         return 0
 
     lax.fori_loop(0, pairs, backward_pair, 0)
 
-    for copy in local + y_moves:
+    for copy in y_moves:
         copy.wait()
-    dx_moves = []
-    for d in range(count):
+    dx_moves = whole_back(1, dx_back)
+    for d in reversed(range(count)):
         tile = tile_of(d)
+        slope = sum(dot(made[tile, :], w_qkv[t], NTRANS) for t, made in enumerate((q, k, v)))
         value = x_in[tile, :].astype(F32)
         inverse = inverse_rms(value)
-        slope = acc[tile, :]
         hat = value * inverse
         gains[0:1, :] += jnp.sum(slope * hat, axis=0, keepdims=True)
-        weighted = slope * gain_one[...]
+        weighted = slope * gain_one[...].reshape(1, features)
         pulled = inverse * (weighted - hat * jnp.mean(weighted * hat, axis=-1, keepdims=True))
         sent[tile, :] = (d_one[tile, :] + pulled).astype(BF)
-        if d == 0:
-            copy = pltpu.make_async_copy(sent.at[tile], dx_back.at[seq], own_sem.at[1])
-        else:
-            copy = to_peer(1, d, sent.at[tile], dx_back.at[seq])
+    for copy in dx_moves[:2]:
         copy.start()
-        dx_moves.append(copy)
 
     axes = links.all()
 
@@ -487,8 +509,8 @@
             src_ref=gains, dst_ref=gains_in.at[i], send_sem=gain_send.at[i], recv_sem=gain_recv.at[i],
             device_id=axes[i], device_id_type=MESH)
 
-    begin = out_chunk + 1 + pairs
-    last = first + 2 * (groups - 1) + reducer.steps - 1
+    begin = out_chunk + 1 + 2 * pairs
+    last = late_down + 4 * (groups - 1) + GAP * (down + reducer.n + 1)
 
     def tail(r, _):
         for i in range(len(axes) + 1):
@@ -501,10 +523,15 @@
                 if i < len(axes):
                     gain_copy(i).start()
 
-        reducer.round(r, plan, finish)
+        advance(r)
+
+        @pl.when(r < begin + X_PIECES)
+        def _():
+            piece_back(1, dx_back, r - begin, X_PIECES)
+
         return 0
 
-    lax.fori_loop(begin, max(last + 1, begin + len(axes) + 1), tail, 0)
+    lax.fori_loop(begin, max(last + 1, begin + max(len(axes) + 1, X_PIECES)), tail, 0)
     gain_sums[...] = gains[...]
     for copy in dx_moves:
         copy.wait()
@@ -512,7 +539,7 @@
         pltpu.make_async_copy(grads.at[c], summed.at[c], out_sem.at[c]).wait()
 
 
-def run_layer(row_bits, blocks, ids, cotangent, w_qkv, w_out, gain_one, gain_two, w_gate, w_up, w_down):
+def run_layer(row_bits, blocks, ids, cotangent, w_query, w_key, w_value, w_out, gain_one, gain_two, w_gate, w_up, w_down):
     count, positions, features = blocks.shape
     hidden = w_gate.shape[1]
     tokens, heads = count * positions, features // HEAD_DIM
@@ -528,11 +555,11 @@
     return pl.pallas_call(
         partial(layer_kernel, row_bits, sizes),
         out_shape=(back, back, jax.ShapeDtypeStruct((chunks, NT, 2, PIECE, 128), BF), jax.ShapeDtypeStruct((8, features), F32)),
-        in_specs=[anywhere] * 5 + [inside] * 2 + [anywhere] * 3,
+        in_specs=[anywhere] * 7 + [inside] * 2 + [anywhere] * 3,
         out_specs=[anywhere] * 3 + [inside],
         scratch_shapes=[
             low, low,
-            pltpu.VMEM((count * 8, positions), jnp.int32), pltpu.VMEM((8, tokens), jnp.int32), pltpu.VMEM((tokens, 128), jnp.int32),
+            pltpu.VMEM((count, count, positions), jnp.int32), pltpu.VMEM((8, tokens), jnp.int32), pltpu.VMEM((tokens, 128), jnp.int32),
             turned, low, low, low, turned, pltpu.VMEM((heads, 8, tokens), F32), full, low, turned, full, full, low,
             pltpu.VMEM((NT, tokens, COLS), BF),
             pltpu.VMEM((3, features, features), BF), pltpu.VMEM((features, features), BF),
@@ -544,7 +571,7 @@
         ],
         compiler_params=pltpu.CompilerParams(collective_id=0, has_side_effects=True, vmem_limit_bytes=63 * 2**20),
         cost_estimate=pl.CostEstimate(flops=60 * 10**9, bytes_accessed=60 * 10**6, transcendentals=10**7),
-    )(blocks, ids, cotangent, w_qkv, w_out, gain_one, gain_two, w_gate, w_up, w_down)
+    )(blocks, ids, cotangent, w_query, w_key, w_value, w_out, gain_one, gain_two, w_gate, w_up, w_down)
 
 
 def widen_ff_kernel(low, gate, up, down):
@@ -589,12 +616,9 @@
 
 
 def body(row_bits, blocks, segment_ids, cotangent, w_query, w_key, w_value, w_out, norm_one, norm_two, w_gate, w_up, w_down):
-    count, positions, features = blocks.shape
-    hidden = w_gate.shape[1]
-    ids = jnp.broadcast_to(segment_ids[:, None, :], (count, 8, positions))
+    features, hidden = w_gate.shape
     y, dx, summed, gains = run_layer(
-        row_bits, blocks, ids, cotangent, jnp.stack([w_query, w_key, w_value]), w_out,
-        norm_one.reshape(1, features), norm_two.reshape(1, features), w_gate, w_up, w_down)
+        row_bits, blocks, segment_ids, cotangent, w_query, w_key, w_value, w_out, norm_one, norm_two, w_gate, w_up, w_down)
     g_gate, g_up, g_down = widen_ff(summed, features, hidden)
     g_out, g_q, g_k, g_v = widen_square(summed, features, hidden // COLS)
     return (y, dx, g_q, g_k, g_v, g_out, gains[0], gains[1], g_gate, g_up, g_down)

time: 255 us -> 222 us (0.87)
  Pallas kernels: 242 us -> 216 us
  local copies, waits for them, and re-layouts: 8.38 us -> 4.55 us
  other arithmetic: 3.4 us -> 0 us
    pallas_call x1, Pallas kernels: 225 us -> 199 us  [run_layer(): pl.pallas_call(partial(layer_kernel, row_bits, sizes), out_shape=(back, b...]
    another operation x1 -> x0, other arithmetic: 3.4 us -> none  [body(): jnp.stack([w_query, w_key, w_value])]
where the time goes in v3:
time: 222 us
  Pallas kernels  216 us (97%)
  local copies, waits for them, and re-layouts  4.55 us (2%)
    pallas_call x1, Pallas kernels, run_layer(): pl.pallas_call(partial(layer_kernel, row_bits, sizes), out_shape=(back, b...  199 us
    pallas_call x1, Pallas kernels, widen_ff(): pl.pallas_call(widen_ff_kernel, grid=(hidden // COLS,), out_shape=(jax.Sh...  11.3 us
    pallas_call x1, Pallas kernels, widen_square(): pl.pallas_call(widen_square_kernel, grid=(features // COLS,), out_shape=(...  6.06 us

profile of v3, /device:TPU:0, one launch (start us, length us, event | category | flops | bytes accessed | tf_op | source)
XLA Modules:
  0.0 221.7 jit_solution(2687079448486703831)
XLA Ops:
  0.6 199.1 %shard_map.203 = (bf16[4,256,768]{2,1,0:T(8,128)(2,1)}, bf16[4,256,768]{2,1,0:T(8,128)(2,1)}, bf16[12,3,2,768,128]{4,3,2,1,0:T(8,128)(2,1)}, f32[8,768]{1,0:T(8,128)}) custom-call(bf16[4,256,768]{2,1,0:T(8,128)(2,1)} %blocks.1, s32[4,256]{1,0:T(4,128)} %ids.1, bf16[4,256,768]{2,1,0:T(8,128)(2,1)} %cotangent.1, bf16[768,768]{1,0:T(8,128)(2,1)} %w_q_hbm.1, ...), custom_call_target="tpu_custom_call" | custom-call | flops 60000002048 | bytes 60000000 | tf_op jit(solution)/shard_map/pallas_call | solution.py:555
  199.8 1.4 slice_reduce_fusion
  201.2 6.1 %shard_map.204 = (f32[768,768]{1,0:T(8,128)}, f32[768,768]{1,0:T(8,128)}, f32[768,768]{1,0:T(8,128)}, f32[768,768]{1,0:T(8,128)}) custom-call(bf16[12,3,2,768,128]{4,3,2,1,0:T(8,128)(2,1)} %get-tuple-element.24.low_out.low_qkv.low, bf16[12,3,2,768,128]{4,3,2,1,0:T(8,128)(2,1)} %get-tuple-element.24.low_out.low_qkv.low), custom_call_target="tpu_custom_call" | custom-call | tf_op jit(solution)/shard_map/pallas_call | solution.py:606
  207.3 0.0 copy-start.1
  207.3 11.3 %shard_map.205 = (f32[768,2048]{1,0:T(8,128)}, f32[768,2048]{1,0:T(8,128)}, f32[2048,768]{1,0:T(8,128)}) custom-call(bf16[12,3,2,768,128]{4,3,2,1,0:T(8,128)(2,1)} %get-tuple-element.24.low_out.low_qkv.low), custom_call_target="tpu_custom_call" | custom-call | tf_op jit(solution)/shard_map/pallas_call | solution.py:587
  218.5 0.0 copy-start
  218.5 0.0 copy-done.1
  218.5 1.1 copy.25
  219.7 0.8 copy-done
  220.5 1.1 copy.26
Async XLA Ops:
  207.3 11.3 %copy-start.1 = (bf16[4,256,768]{2,1,0:T(8,128)(2,1)S(1)}, bf16[4,256,768]{2,1,0:T(8,128)(2,1)}, u32[]{:S(2)}) copy-start(bf16[4,256,768]{2,1,0:T(8,128)(2,1)} %get-tuple-element.46) | copy-start | bytes 4718596
  218.5 2.0 copy-start

commit v4 on v3

--- a/solution.py
+++ b/solution.py
@@ -164,22 +164,16 @@
             c, valid = plan(u - GAP * k)
             pl.when(valid)(partial(self.shrink, k, c))
 
-    def spread_round(self, u, plan, finish):
+    def spread_round(self, u, plan):
         for j in reversed(range(self.n + 2)):
             c, valid = plan(u - GAP * j)
-
-            @pl.when(valid)
-            def _():
-                self.spread(j, c)
-                if j == self.n + 1:
-                    finish(c)
-
-
-def reducer_scratch(row_bits, chunks):
+            pl.when(valid)(partial(self.spread, j, c))
+
+
+def reducer_scratch(row_bits):
     n, e = min(3, row_bits + 1), max(0, row_bits - 2)
     stages = 2 + 2 * n + e
     return [
-        pltpu.VMEM((chunks, NT, 2, PIECE, 128), BF),
         pltpu.VMEM((SLOTS, NT, 2 * PIECE - (PIECE >> n), 128), BF),
         pltpu.VMEM((SLOTS, max(e, 1), NT, PIECE >> n, 128), BF),
         pltpu.SemaphoreType.DMA((SLOTS, stages, NT)),
@@ -200,11 +194,11 @@
 def layer_kernel(
     row_bits, sizes,
     blocks, ids, cotangent, w_q_hbm, w_k_hbm, w_v_hbm, w_out_hbm, gain_one, gain_two, w_gate, w_up, w_down,
-    y_back, dx_back, summed, gain_sums,
-    x_in, g_in, id_rows, id_q, id_k, n1_t, q, k, v, o_t, lse, x_one, n2, n2_t, acc, d_one, sent, part, w_qkv, w_out, gate_buf, up_buf, down_buf,
+    y_back, dx_back, grads, gain_sums,
+    x_in, g_in, id_rows, id_q, id_k, n1_t, q, k, v, o_t, lse, x_one, n2, n2_t, acc, d_one, sent, d_both, h_low, w_qkv, w_out, both_buf, down_buf,
     dk_acc, dv_acc, gains, gains_in,
-    grads, landing, small, send, recv, free,
-    w_sem, ff_sem, own_sem, row_send, row_recv, out_sem, gain_send, gain_recv,
+    landing, small, send, recv, free,
+    w_sem, ff_sem, own_sem, row_send, row_recv, gain_send, gain_recv,
 ):
     tokens, positions, features, hidden, heads = sizes
     ff_chunks, groups, pairs = hidden // COLS, features // COLS, heads // 2
@@ -218,15 +212,17 @@
     reducer = Reducer(links, grads, landing, small, send, recv, free)
 
     def tile_of(d):
-        return pl.ds(pl.multiple_of(links.peers[d] * positions, positions), positions)
+        return slice(positions * d, positions * (d + 1))
+
+    def part_of(ref, d):
+        return ref.at[pl.ds(positions * d, positions)]
 
     loads = [pltpu.make_async_copy(w, w_qkv.at[i], w_sem.at[i]) for i, w in enumerate((w_q_hbm, w_k_hbm, w_v_hbm))]
     loads.append(pltpu.make_async_copy(w_out_hbm, w_out, w_sem.at[3]))
-    mine = tile_of(0)
     own = [
-        pltpu.make_async_copy(blocks.at[seq], x_in.at[mine], own_sem.at[0]),
-        pltpu.make_async_copy(ids, id_rows.at[seq], own_sem.at[1]),
-        pltpu.make_async_copy(cotangent.at[seq], g_in.at[mine], own_sem.at[2]),
+        pltpu.make_async_copy(blocks.at[seq], part_of(x_in, 0), own_sem.at[0]),
+        pltpu.make_async_copy(ids, id_rows.at[0], own_sem.at[1]),
+        pltpu.make_async_copy(cotangent.at[seq], part_of(g_in, 0), own_sem.at[2]),
     ]
     own[0].start()
     for copy in loads:
@@ -240,21 +236,13 @@
             src_ref=src, dst_ref=dst, send_sem=row_send.at[a, d], recv_sem=row_recv.at[a, d],
             device_id=(links.peers[d], row), device_id_type=MESH)
 
-    x_moves = [to_peer(0, d, blocks.at[links.peers[d]], x_in.at[mine]) for d in range(1, count)]
-    id_moves = [to_peer(1, d, ids, id_rows.at[seq]) for d in range(1, count)]
-    g_moves = [to_peer(2, d, cotangent.at[links.peers[d]], g_in.at[mine]) for d in range(1, count)]
-    for copy in x_moves + id_moves:
+    x_moves = [to_peer(0, d, blocks.at[links.peers[d]], part_of(x_in, d)) for d in range(1, count)]
+    id_moves = [to_peer(1, d, ids, id_rows.at[d]) for d in range(1, count)]
+    g_moves = [to_peer(2, d, cotangent.at[links.peers[d]], part_of(g_in, d)) for d in range(1, count)]
+    for copy in id_moves + x_moves + g_moves:
         copy.start()
 
-    own[0].wait()
-    for copy in loads[:3]:
-        copy.wait()
-    for d in range(count):
-        if d > 0:
-            x_moves[d - 1].wait()
-        if d == count - 1:
-            for copy in g_moves:
-                copy.start()
+    def project(d):
         tile = tile_of(d)
         value = x_in[tile, :].astype(F32)
         normed = (value * inverse_rms(value) * gain_one[...].reshape(1, features)).astype(BF)
@@ -262,43 +250,99 @@
         for i, made in enumerate((q, k, v)):
             made[tile, :] = dot(normed, w_qkv[i]).astype(BF)
 
+    own[0].wait()
+    for copy in loads[:3]:
+        copy.wait()
+    project(0)
+    x_moves[0].wait()
+    project(1)
+
     own[1].wait()
     for copy in id_moves:
         copy.wait()
     for d in range(count):
-        id_q[0:1, positions * d : positions * (d + 1)] = id_rows[d, pl.ds(seq, 1), :]
+        id_q[0:1, tile_of(d)] = id_rows[d, pl.ds(seq, 1), :]
     for j in range(tokens // 128):
         block = jnp.broadcast_to(id_q[0:1, 128 * j : 128 * j + 128], (128, 128))
         id_k[128 * j : 128 * j + 128, :] = block.T
 
-    def masked(scores, queries, width):
-        same = jnp.concatenate([id_k[...]] * (width // 128), axis=1) == id_q[0:1, queries]
+    def scores_of(key, keys, queries, cols):
+        width = queries.stop - queries.start
+        scores = dot(key, q[queries, cols], NTRANS) * scale_two
+        same = jnp.concatenate([id_k[keys, :]] * (width // 128), axis=1) == id_q[0:1, queries]
         return jnp.where(same, scores, MASKED)
 
-    def forward_pair(p, _):
+    o_part = d_one
+
+    def attend(blocks, p, _):
         cols = pl.ds(pl.multiple_of(p * 128, 128), 128)
-        key_pair = k[:, cols]
-        value_t = v[:, cols].T
-        for h in range(2):
-            key = half_of(key_pair, h)
-            rows = pl.ds(pl.multiple_of(p * 128 + HEAD_DIM * h, HEAD_DIM), HEAD_DIM)
-            scores = masked(dot(key, q[:, cols], NTRANS) * scale_two, slice(None), tokens)
+        used = slice(0, max(keys.stop for keys, _, _, _ in blocks))
+        key_pair = k[used, cols]
+        value_t = v[used, cols].T
+        sides = [half_of(key_pair, h) for h in range(2)]
+        work = [(h,) + block for block in blocks for h in range(2)]
+
+        def score(h, keys, queries, joined, final):
+            return scores_of(sides[h][keys], keys, queries, cols)
+
+        def weigh(scores, h, keys, queries, joined, final):
+            at = p * 2 + h
             largest = jnp.max(scores, axis=0, keepdims=True)
+            kept = None
+            if joined:
+                before = lse[at, 0:1, queries]
+                largest = jnp.maximum(before, largest)
+                kept = jnp.exp2(before - largest)
             exponent = jnp.exp2(scores - largest)
             total = jnp.sum(exponent, axis=0, keepdims=True)
-            mixed = dot(value_t[HEAD_DIM * h : HEAD_DIM * (h + 1)], exponent.astype(BF))
-            o_t[rows, :] = (mixed / total).astype(BF)
-            lse[p * 2 + h, 0:1, :] = largest + jnp.log2(total)
+            if joined:
+                total += lse[at, 1:2, queries] * kept
+            if final:
+                lse[at, 0:1, queries] = largest + jnp.log2(total)
+            else:
+                lse[at, 0:1, queries] = largest
+                lse[at, 1:2, queries] = total
+            return exponent.astype(BF), total, kept
+
+        def mix(weights, h, keys, queries, joined, final):
+            exponent, total, kept = weights
+            rows = pl.ds(pl.multiple_of(p * 128 + HEAD_DIM * h, HEAD_DIM), HEAD_DIM)
+            mixed = dot(value_t[HEAD_DIM * h : HEAD_DIM * (h + 1), keys], exponent)
+            if joined:
+                mixed += o_part[rows, queries] * kept
+            if final:
+                o_t[rows, queries] = (mixed / total).astype(BF)
+            else:
+                o_part[rows, queries] = mixed
+
+        scores, behind = score(*work[0]), None
+        for i, block in enumerate(work):
+            ahead = score(*work[i + 1]) if i + 1 < len(work) else None
+            weights = weigh(scores, *block)
+            if behind is not None:
+                mix(behind[0], *behind[1])
+            scores, behind = ahead, (weights, block)
+        mix(behind[0], *behind[1])
         return 0
 
-    lax.fori_loop(0, pairs, forward_pair, 0)
+    ends = [positions * d for d in range(count + 1)]
+    lax.fori_loop(0, pairs, partial(attend, [(slice(0, ends[2]), slice(0, ends[2]), False, False)]), 0)
+    x_moves[1].wait()
+    project(2)
+    third, fourth = slice(ends[2], ends[3]), slice(ends[3], ends[4])
+    lax.fori_loop(0, pairs, partial(attend, [
+        (slice(0, ends[3]), third, False, False), (third, slice(0, ends[2]), True, False)]), 0)
+    x_moves[2].wait()
+    project(3)
+    lax.fori_loop(0, pairs, partial(attend, [
+        (slice(0, ends[4]), fourth, False, True), (fourth, slice(0, ends[3]), True, True)]), 0)
 
     def ff_loads(c):
         slot = lax.rem(c, 2)
         cols = pl.ds(pl.multiple_of(c * COLS, COLS), COLS)
         return [
-            pltpu.make_async_copy(w_gate.at[:, cols], gate_buf.at[slot], ff_sem.at[slot, 0]),
-            pltpu.make_async_copy(w_up.at[:, cols], up_buf.at[slot], ff_sem.at[slot, 1]),
+            pltpu.make_async_copy(w_gate.at[:, cols], both_buf.at[slot, :, pl.ds(0, COLS)], ff_sem.at[slot, 0]),
+            pltpu.make_async_copy(w_up.at[:, cols], both_buf.at[slot, :, pl.ds(COLS, COLS)], ff_sem.at[slot, 1]),
             pltpu.make_async_copy(w_down.at[cols, :], down_buf.at[slot], ff_sem.at[slot, 2]),
         ]
 
@@ -338,10 +382,7 @@
 
     def advance(u):
         reducer.shrink_round(u, shrink_plan)
-        reducer.spread_round(u, spread_plan, finish)
-
-    def finish(c):
-        pltpu.make_async_copy(grads.at[c], summed.at[c], out_sem.at[c]).start()
+        reducer.spread_round(u, spread_plan)
 
     def put(c, t, piece):
         for half in range(2):
@@ -361,8 +402,8 @@
             copy.wait()
         for i in range(2):
             tile = slice(half_tokens * i, half_tokens * (i + 1))
-            gate = dot(n2[tile, :], gate_buf[slot])
-            up = dot(n2[tile, :], up_buf[slot])
+            both = dot(n2[tile, :], both_buf[slot])
+            gate, up = both[:, :COLS], both[:, COLS:]
             d_hidden = dot(g_in[tile, :], down_buf[slot], NTRANS)
             square = gate * gate
             bend = 0.7978845608028654 * 0.044715
@@ -371,16 +412,15 @@
             activated = gate * rise
             slope = rise + 0.5 * gate * (1.0 - turn * turn) * (0.7978845608028654 + 3.0 * bend * square)
             low_h = (activated * up).astype(BF)
-            low_gate = (d_hidden * up * slope).astype(BF)
-            low_up = (d_hidden * activated).astype(BF)
-            part[0, tile, :] = low_gate
-            part[1, tile, :] = low_up
-            part[2, tile, :] = low_h
+            low_both = jnp.concatenate([(d_hidden * up * slope).astype(BF), (d_hidden * activated).astype(BF)], axis=1)
+            d_both[tile, :] = low_both
+            h_low[tile, :] = low_h
             acc[tile, :] += dot(low_h, down_buf[slot])
-            d_one[tile, :] += dot(low_gate, gate_buf[slot], NTRANS) + dot(low_up, up_buf[slot], NTRANS)
-        put(c, 0, dot(n2_t[...], part[0]))
-        put(c, 1, dot(n2_t[...], part[1]))
-        made = dot(part[2].T, g_in[...])
+            d_one[tile, :] += dot(low_both, both_buf[slot], NTRANS)
+        made = dot(n2_t[...], d_both[...])
+        put(c, 0, made[:, :COLS])
+        put(c, 1, made[:, COLS:])
+        made = dot(h_low[...].T, g_in[...])
         for j in range(NT):
             for half in range(2):
                 at = COLS * j + 128 * half
@@ -396,13 +436,13 @@
         sent[tile, :] = acc[tile, :].astype(BF)
 
     def whole_back(a, dst):
-        own_copy = pltpu.make_async_copy(sent.at[mine], dst.at[seq], own_sem.at[a])
-        return [own_copy] + [to_peer(a, d, sent.at[tile_of(d)], dst.at[seq]) for d in range(1, count)]
+        own_copy = pltpu.make_async_copy(part_of(sent, 0), dst.at[seq], own_sem.at[a])
+        return [own_copy] + [to_peer(a, d, part_of(sent, d), dst.at[seq]) for d in range(1, count)]
 
     def piece_back(a, dst, i, pieces):
         rows = positions // pieces
         for d in range(2, count):
-            low = pl.multiple_of(links.peers[d] * positions + i * rows, 16)
+            low = pl.multiple_of(positions * d + i * rows, 16)
             to = pl.ds(pl.multiple_of(i * rows, 16), rows)
             to_peer(a, d, sent.at[pl.ds(low, rows)], dst.at[seq, to]).start()
 
@@ -443,7 +483,7 @@
             dq_parts = []
             for i in range(tokens // width):
                 qs = slice(width * i, width * (i + 1))
-                scores = masked(dot(key, q[qs, cols], NTRANS) * scale_two, qs, width)
+                scores = scores_of(key, slice(0, tokens), qs, cols)
                 prob = jnp.exp2(scores - lse[step * 2 + h, 0:1, qs])
                 delta = jnp.sum(n2_t[rows, qs].astype(F32) * o_t[rows, qs].astype(F32), axis=0, keepdims=True)
                 d_prob = dot(value, n2[qs, cols], NTRANS)
@@ -535,8 +575,6 @@
     gain_sums[...] = gains[...]
     for copy in dx_moves:
         copy.wait()
-    for c in range(chunks):
-        pltpu.make_async_copy(grads.at[c], summed.at[c], out_sem.at[c]).wait()
 
 
 def run_layer(row_bits, blocks, ids, cotangent, w_query, w_key, w_value, w_out, gain_one, gain_two, w_gate, w_up, w_down):
@@ -554,74 +592,101 @@
     dma = pltpu.SemaphoreType.DMA
     return pl.pallas_call(
         partial(layer_kernel, row_bits, sizes),
-        out_shape=(back, back, jax.ShapeDtypeStruct((chunks, NT, 2, PIECE, 128), BF), jax.ShapeDtypeStruct((8, features), F32)),
+        out_shape=(back, back, pltpu.VMEM((chunks, NT, 2, PIECE, 128), BF), jax.ShapeDtypeStruct((8, features), F32)),
         in_specs=[anywhere] * 7 + [inside] * 2 + [anywhere] * 3,
-        out_specs=[anywhere] * 3 + [inside],
+        out_specs=[anywhere] * 2 + [inside] * 2,
         scratch_shapes=[
             low, low,
             pltpu.VMEM((count, count, positions), jnp.int32), pltpu.VMEM((8, tokens), jnp.int32), pltpu.VMEM((tokens, 128), jnp.int32),
             turned, low, low, low, turned, pltpu.VMEM((heads, 8, tokens), F32), full, low, turned, full, full, low,
-            pltpu.VMEM((NT, tokens, COLS), BF),
+            pltpu.VMEM((tokens, 2 * COLS), BF), pltpu.VMEM((tokens, COLS), BF),
             pltpu.VMEM((3, features, features), BF), pltpu.VMEM((features, features), BF),
-            pltpu.VMEM((2, features, COLS), BF), pltpu.VMEM((2, features, COLS), BF), pltpu.VMEM((2, COLS, features), BF),
+            pltpu.VMEM((2, features, 2 * COLS), BF), pltpu.VMEM((2, COLS, features), BF),
             pltpu.VMEM((2, tokens, 128), F32), pltpu.VMEM((2, tokens, 128), F32),
             pltpu.VMEM((8, features), F32), pltpu.VMEM((axes, 8, features), F32),
-        ] + reducer_scratch(row_bits, chunks) + [
-            dma((4,)), dma((2, 3)), dma((3,)), dma((3, count)), dma((3, count)), dma((chunks,)), dma((axes,)), dma((axes,)),
+        ] + reducer_scratch(row_bits) + [
+            dma((4,)), dma((2, 3)), dma((3,)), dma((3, count)), dma((3, count)), dma((axes,)), dma((axes,)),
         ],
-        compiler_params=pltpu.CompilerParams(collective_id=0, has_side_effects=True, vmem_limit_bytes=63 * 2**20),
+        compiler_params=pltpu.CompilerParams(collective_id=0, has_side_effects=True, vmem_limit_bytes=49 * 2**20),
         cost_estimate=pl.CostEstimate(flops=60 * 10**9, bytes_accessed=60 * 10**6, transcendentals=10**7),
     )(blocks, ids, cotangent, w_query, w_key, w_value, w_out, gain_one, gain_two, w_gate, w_up, w_down)
 
 
-def widen_ff_kernel(low, gate, up, down):
-    for half in range(2):
-        cols = slice(128 * half, 128 * half + 128)
-        gate[:, cols] = low[0, 0, half].astype(F32)
-        up[:, cols] = low[0, 1, half].astype(F32)
-        for j in range(NT):
-            down[:, COLS * j + 128 * half : COLS * j + 128 * half + 128] = low[0, 2, half, COLS * j : COLS * (j + 1), :].astype(F32)
-
-
-def widen_ff(summed, features, hidden):
+def widen_kernel(
+    ff_chunks, groups,
+    low, y_in, dx_in, gain_sums,
+    y, dx, g_q, g_k, g_v, g_out, g_one, g_two, g_gate, g_up, g_down,
+    wide, wide_down, held, out_sem, move_sem,
+):
+    chunks = ff_chunks + 1 + groups
+    arrive = [pltpu.make_async_copy(src, held.at[i], move_sem.at[0, i]) for i, src in enumerate((y_in, dx_in))]
+    leave = [pltpu.make_async_copy(held.at[i], dst, move_sem.at[1, i]) for i, dst in enumerate((y, dx))]
+
+    def stores(c):
+        slot = c % 2
+        cols = pl.ds(COLS * c, COLS)
+        if c < ff_chunks:
+            pairs = [(wide.at[slot, 0], g_gate.at[:, cols]), (wide.at[slot, 1], g_up.at[:, cols]), (wide_down.at[slot], g_down.at[cols, :])]
+        elif c == ff_chunks:
+            pairs = [(wide.at[slot, t], g_out.at[:, pl.ds(COLS * t, COLS)]) for t in range(NT)]
+        else:
+            cols = pl.ds(COLS * (c - ff_chunks - 1), COLS)
+            pairs = [(wide.at[slot, t], made.at[:, cols]) for t, made in enumerate((g_q, g_k, g_v))]
+        return [pltpu.make_async_copy(src, dst, out_sem.at[slot, t]) for t, (src, dst) in enumerate(pairs)]
+
+    for copy in arrive:
+        copy.start()
+    g_one[...] = gain_sums[0, :]
+    g_two[...] = gain_sums[1, :]
+    for c in range(chunks):
+        if c >= 2:
+            for copy in stores(c - 2):
+                copy.wait()
+        for half in range(2):
+            cols = slice(128 * half, 128 * half + 128)
+            for t in range(NT):
+                if t == 2 and c < ff_chunks:
+                    for j in range(NT):
+                        at = COLS * j + 128 * half
+                        wide_down[c % 2, :, at : at + 128] = low[c, t, half, COLS * j : COLS * (j + 1), :].astype(F32)
+                else:
+                    wide[c % 2, t, :, cols] = low[c, t, half].astype(F32)
+        for copy in stores(c):
+            copy.start()
+        if c < 2:
+            arrive[c].wait()
+            leave[c].start()
+    for c in range(chunks - 2, chunks):
+        for copy in stores(c):
+            copy.wait()
+    for copy in leave:
+        copy.wait()
+
+
+def widen(summed, y, dx, gains, features, hidden):
+    anywhere, inside = pl.BlockSpec(memory_space=pl.ANY), pl.BlockSpec(memory_space=pltpu.VMEM)
+    square, gain = jax.ShapeDtypeStruct((features, features), F32), jax.ShapeDtypeStruct((features,), F32)
+    flat, tall = jax.ShapeDtypeStruct((features, hidden), F32), jax.ShapeDtypeStruct((hidden, features), F32)
+    back = jax.ShapeDtypeStruct(y.shape, y.dtype)
+    dma = pltpu.SemaphoreType.DMA
     return pl.pallas_call(
-        widen_ff_kernel,
-        grid=(hidden // COLS,),
-        out_shape=(jax.ShapeDtypeStruct((features, hidden), F32),) * 2 + (jax.ShapeDtypeStruct((hidden, features), F32),),
-        in_specs=[pl.BlockSpec((1, NT, 2, PIECE, 128), lambda c: (c, 0, 0, 0, 0))],
-        out_specs=[pl.BlockSpec((features, COLS), lambda c: (0, c))] * 2 + [pl.BlockSpec((COLS, features), lambda c: (c, 0))],
-    )(summed)
-
-
-def widen_square_kernel(low_out, low_qkv, g_out, g_q, g_k, g_v):
-    for half in range(2):
-        cols = slice(128 * half, 128 * half + 128)
-        g_out[:, cols] = low_out[0, 0, half].astype(F32)
-        for t, made in enumerate((g_q, g_k, g_v)):
-            made[:, cols] = low_qkv[0, t, half].astype(F32)
-
-
-def widen_square(summed, features, first):
-    wide = pl.BlockSpec((features, COLS), lambda j: (0, j))
-    return pl.pallas_call(
-        widen_square_kernel,
-        grid=(features // COLS,),
-        out_shape=(jax.ShapeDtypeStruct((features, features), F32),) * 4,
-        in_specs=[
-            pl.BlockSpec((1, 1, 2, PIECE, 128), lambda j: (first, j, 0, 0, 0)),
-            pl.BlockSpec((1, NT, 2, PIECE, 128), lambda j: (first + 1 + j, 0, 0, 0, 0)),
+        partial(widen_kernel, hidden // COLS, features // COLS),
+        out_shape=(back, back) + (square,) * 4 + (gain,) * 2 + (flat, flat, tall),
+        in_specs=[inside] + [pl.BlockSpec(memory_space=pltpu.HBM)] * 2 + [inside],
+        out_specs=[anywhere] * 6 + [inside] * 2 + [anywhere] * 3,
+        scratch_shapes=[
+            pltpu.VMEM((2, NT, PIECE, COLS), F32), pltpu.VMEM((2, COLS, features), F32), pltpu.VMEM((2,) + y.shape, BF),
+            dma((2, NT)), dma((2, 2)),
         ],
-        out_specs=[wide] * 4,
-    )(summed, summed)
+        compiler_params=pltpu.CompilerParams(vmem_limit_bytes=48 * 2**20),
+    )(pltpu.with_memory_space_constraint(summed, pltpu.VMEM), y, dx, gains)
 
 
 def body(row_bits, blocks, segment_ids, cotangent, w_query, w_key, w_value, w_out, norm_one, norm_two, w_gate, w_up, w_down):
     features, hidden = w_gate.shape
     y, dx, summed, gains = run_layer(
         row_bits, blocks, segment_ids, cotangent, w_query, w_key, w_value, w_out, norm_one, norm_two, w_gate, w_up, w_down)
-    g_gate, g_up, g_down = widen_ff(summed, features, hidden)
-    g_out, g_q, g_k, g_v = widen_square(summed, features, hidden // COLS)
-    return (y, dx, g_q, g_k, g_v, g_out, gains[0], gains[1], g_gate, g_up, g_down)
+    return widen(summed, y, dx, gains, features, hidden)
 
 
 def solution(mesh):

time: 222 us -> 206 us (0.928)
  Pallas kernels: 216 us -> 205 us
  local copies, waits for them, and re-layouts: 4.55 us -> 0 us
    pallas_call x1, Pallas kernels: 199 us -> 192 us  [run_layer(): pl.pallas_call(partial(layer_kernel, row_bits, sizes), out_shape=(back, b...]
    pallas_call x2 -> x1, Pallas kernels: 17.3 us -> 13.5 us  [widen(): pl.pallas_call(partial(widen_kernel, hidden // COLS, features // COLS), o...]
    unnamed x6 -> x0, local copies, waits for them, and re-layouts: 3.12 us -> none
where the time goes in v4:
time: 206 us
  Pallas kernels  205 us (100%)
    pallas_call x1, Pallas kernels, run_layer(): pl.pallas_call(partial(layer_kernel, row_bits, sizes), out_shape=(back, b...  192 us
    pallas_call x1, Pallas kernels, widen(): pl.pallas_call(partial(widen_kernel, hidden // COLS, features // COLS), o...  13.5 us

profile of v4, /device:TPU:0, one launch (start us, length us, event | category | flops | bytes accessed | tf_op | source)
XLA Modules:
  0.0 205.9 jit_solution(9841372109349083372)
XLA Ops:
  0.6 191.5 %shard_map.203 = (bf16[4,256,768]{2,1,0:T(8,128)(2,1)}, bf16[4,256,768]{2,1,0:T(8,128)(2,1)}, bf16[12,3,2,768,128]{4,3,2,1,0:T(8,128)(2,1)S(1)}, f32[8,768]{1,0:T(8,128)}) custom-call(bf16[4,256,768]{2,1,0:T(8,128)(2,1)} %blocks.1, s32[4,256]{1,0:T(4,128)} %ids.1, bf16[4,256,768]{2,1,0:T(8,128)(2,1)} %cotangent.1, bf16[768,768]{1,0:T(8,128)(2,1)} %w_q_hbm.1, ...), custom_call_target="tpu_custom_call" | custom-call | flops 60000002048 | bytes 60000000 | tf_op jit(solution)/shard_map/pallas_call | solution.py:593
  192.2 13.5 %shard_map.204 = (bf16[4,256,768]{2,1,0:T(8,128)(2,1)}, bf16[4,256,768]{2,1,0:T(8,128)(2,1)}, f32[768,768]{1,0:T(8,128)}, f32[768,768]{1,0:T(8,128)}, f32[768,76...) custom-call(bf16[12,3,2,768,128]{4,3,2,1,0:T(8,128)(2,1)S(1)} %get-t, ...), custom_call_target="tpu_custom_call" | custom-call | tf_op jit(solution)/shard_map/pallas_call | solution.py:672

commit v5 on v4

--- a/solution.py
+++ b/solution.py
@@ -51,7 +51,17 @@
         self.extra = dims[3:]
         n = len(self.halving)
         orders = [(0, 1, 2), (1, 2, 0), (2, 0, 1)]
-        self.orders = [[d for d in order if d < n] for order in orders]
+        others = [(1, 0, 2), (1, 2, 0), (2, 0, 1)]
+        self.orders = [[[d for d in order if d < n] for order in both] for both in (orders, others)]
+
+    def level(self, c, t, k):
+        here, there = (both[t][k] for both in self.orders)
+        if here == there:
+            return self.halving[here]
+        even = 1 - lax.rem(c, 2)
+        (own_a, (seq_a, row_a)), (own_b, (seq_b, row_b)) = self.halving[here], self.halving[there]
+        pick = lambda a, b: a + (b - a) * even
+        return pick(own_a, own_b), (pick(seq_a, seq_b), pick(row_a, row_b))
 
     def all(self):
         return [self.other_core] + [p for _, p in self.halving + self.extra]
@@ -71,10 +81,10 @@
         n, e = len(links.halving), len(links.extra)
         self.n, self.e = n, e
 
-    def span(self, t, level):
+    def span(self, c, t, level):
         low = 0
         for k in range(level):
-            low = low + self.l.halving[self.l.orders[t][k]][0] * (PIECE >> (k + 1))
+            low = low + self.l.level(c, t, k)[0] * (PIECE >> (k + 1))
         return low if level == 0 else pl.multiple_of(low, 16)
 
     def copies(self, c, stage):
@@ -86,9 +96,9 @@
         if stage <= n:
             out = []
             for t in range(NT):
-                own, partner = l.halving[l.orders[t][stage - 1]]
+                own, partner = l.level(c, t, stage - 1)
                 rows = PIECE >> stage
-                low = pl.multiple_of(self.span(t, stage - 1) + (1 - own) * rows, 16)
+                low = pl.multiple_of(self.span(c, t, stage - 1) + (1 - own) * rows, 16)
                 src = self.g.at[c, t, core, pl.ds(low, rows)]
                 dst = self.landing.at[slot, t, pl.ds(2 * PIECE - 2 * rows, rows)]
                 out.append(self.make(src, dst, c, stage, t, partner))
@@ -98,15 +108,15 @@
             partner = l.extra[stage - n - 1][1]
             out = []
             for t in range(NT):
-                src = self.g.at[c, t, core, pl.ds(self.span(t, n), rows)]
+                src = self.g.at[c, t, core, pl.ds(self.span(c, t, n), rows)]
                 out.append(self.make(src, self.small.at[slot, stage - n - 1, t], c, stage, t, partner))
             return out
         k = 2 * n + e + 1 - stage
         if k > 0:
             out = []
             for t in range(NT):
-                view = self.g.at[c, t, core, pl.ds(self.span(t, k), PIECE >> k)]
-                out.append(self.make(view, view, c, stage, t, l.halving[l.orders[t][k - 1]][1]))
+                view = self.g.at[c, t, core, pl.ds(self.span(c, t, k), PIECE >> k)]
+                out.append(self.make(view, view, c, stage, t, l.level(c, t, k - 1)[1]))
             return out
         view = self.g.at[c, :, core]
         return [self.make(view, view, c, stage, 0, l.other_core)]
@@ -124,17 +134,17 @@
         core, slot = self.l.core, lax.rem(c, SLOTS)
         rows = PIECE >> min(stage, n)
         for t in range(NT):
-            view = self.g.at[c, t, core, pl.ds(self.span(t, min(stage, n)), rows)]
+            view = self.g.at[c, t, core, pl.ds(self.span(c, t, min(stage, n)), rows)]
             if stage <= n:
                 got = self.landing[slot, t, pl.ds(0 if stage == 0 else 2 * PIECE - 2 * rows, rows)]
             else:
                 got = self.small[slot, stage - n - 1, t]
             view[...] = view[...] + got
 
-    def partners(self, level):
+    def partners(self, c, level):
         if level == 0:
             return [(0, self.l.other_core)]
-        return [(t, self.l.halving[self.l.orders[t][level - 1]][1]) for t in range(NT)]
+        return [(t, self.l.level(c, t, level - 1)[1]) for t in range(NT)]
 
     def shrink(self, k, c):
         if k > 0:
@@ -142,8 +152,8 @@
                 copy.wait()
             self.fold(c, k - 1)
             if k - 1 <= self.n:
-                for t, partner in self.partners(k - 1):
-                    pl.semaphore_signal(self.free.at[k - 1, t], inc=1, device_id=partner, device_id_type=MESH)
+                for t, partner in self.partners(c, k - 1):
+                    pl.semaphore_signal(self.free.at[k - 1, t, lax.rem(c, 2)], inc=1, device_id=partner, device_id_type=MESH)
         if k <= self.n + self.e:
             for copy in self.copies(c, k):
                 copy.start()
@@ -154,8 +164,8 @@
             for copy in self.copies(c, stage - 1):
                 copy.wait()
         if j <= self.n:
-            for t, _ in self.partners(self.n - j):
-                pl.semaphore_wait(self.free.at[self.n - j, t], 1)
+            for t, _ in self.partners(c, self.n - j):
+                pl.semaphore_wait(self.free.at[self.n - j, t, lax.rem(c, 2)], 1)
             for copy in self.copies(c, stage):
                 copy.start()
 
@@ -178,7 +188,7 @@
         pltpu.VMEM((SLOTS, max(e, 1), NT, PIECE >> n, 128), BF),
         pltpu.SemaphoreType.DMA((SLOTS, stages, NT)),
         pltpu.SemaphoreType.DMA((SLOTS, stages, NT)),
-        pltpu.SemaphoreType.REGULAR((n + 1, NT)),
+        pltpu.SemaphoreType.REGULAR((n + 1, NT, 2)),
     ]
 
 
@@ -373,8 +383,9 @@
 
     def shrink_plan(u):
         late = u - late_down
-        chunk = jnp.where(u <= out_chunk, u, out_chunk + 1 + late // 4)
-        valid = (u >= 0) & ((u <= out_chunk) | ((late >= 0) & (late <= 4 * (groups - 1)) & (lax.rem(late, 4) == 0)))
+        chunk = jnp.where(u < out_chunk, u, jnp.where(u == out_chunk + 1, out_chunk, out_chunk + 1 + late // 4))
+        soon = (u >= 0) & ((u < out_chunk) | (u == out_chunk + 1))
+        valid = soon | ((late >= 0) & (late <= 4 * (groups - 1)) & (lax.rem(late, 4) == 0))
         return chunk, valid
 
     def spread_plan(u):
@@ -465,11 +476,12 @@
         d_mixed = dot(low, w_out[...], NTRANS).astype(BF)
         n2[tile, :] = d_mixed
         n2_t[:, tile] = d_mixed.T
-    for t in range(NT):
-        put(out_chunk, t, dot(o_t[...], g_in[:, COLS * t : COLS * (t + 1)]))
     reducer.shrink_round(jnp.int32(out_chunk), shrink_plan)
 
     width = 256
+
+    def slope_of(tile, group):
+        return sum(dot(made[tile, group], w_qkv[t, :, group], NTRANS) for t, made in enumerate((q, k, v)))
 
     def backward_pair(step, _):
         g, j = step // 2, lax.rem(step, 2)
@@ -500,6 +512,12 @@
                 dq_parts.append((dot(key_t[HEAD_DIM * h : HEAD_DIM * (h + 1)], d_score) * scale).astype(BF))
             dq.append(jnp.concatenate(dq_parts, axis=1))
             if h == 0:
+
+                @pl.when(step == 0)
+                def _():
+                    for t in range(NT):
+                        put(out_chunk, t, dot(o_t[...], g_in[:, COLS * t : COLS * (t + 1)]))
+
                 advance(out_chunk + 1 + 2 * step)
 
                 @pl.when(step < Y_PIECES // 2)
@@ -522,6 +540,12 @@
         def _():
             piece_back(0, y_back, 2 * step + 1, Y_PIECES)
 
+        @pl.when((j == 1) & (g < groups - 1))
+        def _():
+            for d in range(count):
+                back = slope_of(tile_of(d), pl.ds(pl.multiple_of(g * COLS, COLS), COLS))
+                acc[tile_of(d), :] = jnp.where(g == 0, back, acc[tile_of(d), :] + back)
+
         return 0
 
     lax.fori_loop(0, pairs, backward_pair, 0)
@@ -531,7 +555,7 @@
     dx_moves = whole_back(1, dx_back)
     for d in reversed(range(count)):
         tile = tile_of(d)
-        slope = sum(dot(made[tile, :], w_qkv[t], NTRANS) for t, made in enumerate((q, k, v)))
+        slope = acc[tile, :] + slope_of(tile, slice(features - COLS, features))
         value = x_in[tile, :].astype(F32)
         inverse = inverse_rms(value)
         hat = value * inverse
@@ -623,7 +647,7 @@
     leave = [pltpu.make_async_copy(held.at[i], dst, move_sem.at[1, i]) for i, dst in enumerate((y, dx))]
 
     def stores(c):
-        slot = c % 2
+        slot = c % 3
         cols = pl.ds(COLS * c, COLS)
         if c < ff_chunks:
             pairs = [(wide.at[slot, 0], g_gate.at[:, cols]), (wide.at[slot, 1], g_up.at[:, cols]), (wide_down.at[slot], g_down.at[cols, :])]
@@ -639,8 +663,8 @@
     g_one[...] = gain_sums[0, :]
     g_two[...] = gain_sums[1, :]
     for c in range(chunks):
-        if c >= 2:
-            for copy in stores(c - 2):
+        if c >= 3:
+            for copy in stores(c - 3):
                 copy.wait()
         for half in range(2):
             cols = slice(128 * half, 128 * half + 128)
@@ -648,15 +672,15 @@
                 if t == 2 and c < ff_chunks:
                     for j in range(NT):
                         at = COLS * j + 128 * half
-                        wide_down[c % 2, :, at : at + 128] = low[c, t, half, COLS * j : COLS * (j + 1), :].astype(F32)
+                        wide_down[c % 3, :, at : at + 128] = low[c, t, half, COLS * j : COLS * (j + 1), :].astype(F32)
                 else:
-                    wide[c % 2, t, :, cols] = low[c, t, half].astype(F32)
+                    wide[c % 3, t, :, cols] = low[c, t, half].astype(F32)
         for copy in stores(c):
             copy.start()
         if c < 2:
             arrive[c].wait()
             leave[c].start()
-    for c in range(chunks - 2, chunks):
+    for c in range(chunks - 3, chunks):
         for copy in stores(c):
             copy.wait()
     for copy in leave:
@@ -675,8 +699,8 @@
         in_specs=[inside] + [pl.BlockSpec(memory_space=pltpu.HBM)] * 2 + [inside],
         out_specs=[anywhere] * 6 + [inside] * 2 + [anywhere] * 3,
         scratch_shapes=[
-            pltpu.VMEM((2, NT, PIECE, COLS), F32), pltpu.VMEM((2, COLS, features), F32), pltpu.VMEM((2,) + y.shape, BF),
-            dma((2, NT)), dma((2, 2)),
+            pltpu.VMEM((3, NT, PIECE, COLS), F32), pltpu.VMEM((3, COLS, features), F32), pltpu.VMEM((2,) + y.shape, BF),
+            dma((3, NT)), dma((2, 2)),
         ],
         compiler_params=pltpu.CompilerParams(vmem_limit_bytes=48 * 2**20),
     )(pltpu.with_memory_space_constraint(summed, pltpu.VMEM), y, dx, gains)

time: 206 us -> 204 us (level)
    pallas_call x1, Pallas kernels: 192 us -> 189 us  [run_layer(): pl.pallas_call(partial(layer_kernel, row_bits, sizes), out_shape=(back, b...]
where the time goes in v5:
time: 204 us
  Pallas kernels  203 us (100%)
    pallas_call x1, Pallas kernels, run_layer(): pl.pallas_call(partial(layer_kernel, row_bits, sizes), out_shape=(back, b...  189 us
    pallas_call x1, Pallas kernels, widen(): pl.pallas_call(partial(widen_kernel, hidden // COLS, features // COLS), o...  13.2 us

profile of v5, /device:TPU:0, one launch (start us, length us, event | category | flops | bytes accessed | tf_op | source)
XLA Modules:
  0.0 203.5 jit_solution(15016713251034131976)
XLA Ops:
  0.6 189.4 %shard_map.203 = (bf16[4,256,768]{2,1,0:T(8,128)(2,1)}, bf16[4,256,768]{2,1,0:T(8,128)(2,1)}, bf16[12,3,2,768,128]{4,3,2,1,0:T(8,128)(2,1)S(1)}, f32[8,768]{1,0:T(8,128)}) custom-call(bf16[4,256,768]{2,1,0:T(8,128)(2,1)} %blocks.1, s32[4,256]{1,0:T(4,128)} %ids.1, bf16[4,256,768]{2,1,0:T(8,128)(2,1)} %cotangent.1, bf16[768,768]{1,0:T(8,128)(2,1)} %w_q_hbm.1, ...), custom_call_target="tpu_custom_call" | custom-call | flops 60000002048 | bytes 60000000 | tf_op jit(solution)/shard_map/pallas_call | solution.py:617
  190.1 13.2 %shard_map.204 = (bf16[4,256,768]{2,1,0:T(8,128)(2,1)}, bf16[4,256,768]{2,1,0:T(8,128)(2,1)}, f32[768,768]{1,0:T(8,128)}, f32[768,768]{1,0:T(8,128)}, f32[768,76...) custom-call(bf16[12,3,2,768,128]{4,3,2,1,0:T(8,128)(2,1)S(1)} %get-t, ...), custom_call_target="tpu_custom_call" | custom-call | tf_op jit(solution)/shard_map/pallas_call | solution.py:696

commit v6 on v5

--- a/solution.py
+++ b/solution.py
@@ -16,7 +16,7 @@
 COLS = 256
 SLOTS = 4
 GAP = 2
-Y_PIECES = 8
+Y_PIECES = 4
 X_PIECES = 16
 BF = jnp.bfloat16
 F32 = jnp.float32

time: 204 us -> 207 us (1.015)
  Pallas kernels: 203 us -> 206 us
    pallas_call x1, Pallas kernels: 189 us -> 193 us  [run_layer(): pl.pallas_call(partial(layer_kernel, row_bits, sizes), out_shape=(back, b...]
where the time goes in v6:
time: 207 us
  Pallas kernels  206 us (100%)
    pallas_call x1, Pallas kernels, run_layer(): pl.pallas_call(partial(layer_kernel, row_bits, sizes), out_shape=(back, b...  193 us
    pallas_call x1, Pallas kernels, widen(): pl.pallas_call(partial(widen_kernel, hidden // COLS, features // COLS), o...  13.2 us

profile of v6, /device:TPU:0, one launch (start us, length us, event | category | flops | bytes accessed | tf_op | source)
XLA Modules:
  0.0 207.3 jit_solution(1948157008468620673)
XLA Ops:
  0.6 193.2 %shard_map.203 = (bf16[4,256,768]{2,1,0:T(8,128)(2,1)}, bf16[4,256,768]{2,1,0:T(8,128)(2,1)}, bf16[12,3,2,768,128]{4,3,2,1,0:T(8,128)(2,1)S(1)}, f32[8,768]{1,0:T(8,128)}) custom-call(bf16[4,256,768]{2,1,0:T(8,128)(2,1)} %blocks.1, s32[4,256]{1,0:T(4,128)} %ids.1, bf16[4,256,768]{2,1,0:T(8,128)(2,1)} %cotangent.1, bf16[768,768]{1,0:T(8,128)(2,1)} %w_q_hbm.1, ...), custom_call_target="tpu_custom_call" | custom-call | flops 60000002048 | bytes 60000000 | tf_op jit(solution)/shard_map/pallas_call | solution.py:617
  193.8 13.2 %shard_map.204 = (bf16[4,256,768]{2,1,0:T(8,128)(2,1)}, bf16[4,256,768]{2,1,0:T(8,128)(2,1)}, f32[768,768]{1,0:T(8,128)}, f32[768,768]{1,0:T(8,128)}, f32[768,76...) custom-call(bf16[12,3,2,768,128]{4,3,2,1,0:T(8,128)(2,1)S(1)} %get-t, ...), custom_call_target="tpu_custom_call" | custom-call | tf_op jit(solution)/shard_map/pallas_call | solution.py:696
